TPU v7x, 32 devices: a whole 2x2x4 slice. The times are simulated.
32 devices in a mesh: res: 2 (over core), dp: 8 (over z, x), fsdp: 2 (over y).
Axes of the slice: x: 2, y: 2, z: 4, core: 2. Of those that a mesh axis runs over, the one named last changes fastest.
Arguments:
- tokens_in: bfloat16 [8192, 1024], P(('res', 'dp', 'fsdp')), may hold values from -6 to 6
- cotangent: bfloat16 [8192, 1024], P(('res', 'dp', 'fsdp')), may hold values from -6 to 6
- crop_counts: int32 [2, 8, 2, 2], P('res', 'dp', 'fsdp'), may hold values from 0 to 20, as said below
- group_tokens: int32 [2], replicated, may hold values from 1024 to 8191
- weight_qkv: float32 [1024, 3072], P('fsdp')
- rows_qkv: float32 [1024], P('fsdp'), may hold values from 655.36 to 5242.88
- cols_qkv: float32 [3072], replicated, may hold values from 655.36 to 5242.88
- weight_out: float32 [1024, 1024], P('fsdp')
- rows_out: float32 [1024], P('fsdp'), may hold values from 81.92 to 655.36
- cols_out: float32 [1024], replicated, may hold values from 81.92 to 655.36
- weight_up: float32 [1024, 4096], P('fsdp')
- rows_up: float32 [1024], P('fsdp'), may hold values from 81.92 to 655.36
- cols_up: float32 [4096], replicated, may hold values from 81.92 to 655.36
- weight_down: float32 [4096, 1024], P('fsdp')
- rows_down: float32 [4096], P('fsdp'), may hold values from 204.8 to 1638.4
- cols_down: float32 [1024], replicated, may hold values from 204.8 to 1638.4
- vectors: float32 [1024, 12], P('fsdp')
- moment_vec: float32 [1024, 12], P('fsdp'), may hold values from 204.8 to 1638.4
Outputs:
- tokens_out: bfloat16 [8192, 1024], P(('res', 'dp', 'fsdp'))
- grad_in: float32 [8192, 1024], P(('res', 'dp', 'fsdp'))
- grad_qkv: float32 [1024, 3072], P('fsdp')
- rows_qkv_new: float32 [1024], P('fsdp')
- cols_qkv_new: float32 [3072], replicated
- weight_qkv_new: float32 [1024, 3072], P('fsdp')
- weight_qkv_half: bfloat16 [1024, 3072], P('fsdp')
- grad_out: float32 [1024, 1024], P('fsdp')
- rows_out_new: float32 [1024], P('fsdp')
- cols_out_new: float32 [1024], replicated
- weight_out_new: float32 [1024, 1024], P('fsdp')
- weight_out_half: bfloat16 [1024, 1024], P('fsdp')
- grad_up: float32 [1024, 4096], P('fsdp')
- rows_up_new: float32 [1024], P('fsdp')
- cols_up_new: float32 [4096], replicated
- weight_up_new: float32 [1024, 4096], P('fsdp')
- weight_up_half: bfloat16 [1024, 4096], P('fsdp')
- grad_down: float32 [4096, 1024], P('fsdp')
- rows_down_new: float32 [4096], P('fsdp')
- cols_down_new: float32 [1024], replicated
- weight_down_new: float32 [4096, 1024], P('fsdp')
- weight_down_half: bfloat16 [4096, 1024], P('fsdp')
- grad_vectors: float32 [1024, 12], P('fsdp')
- moment_vec_new: float32 [1024, 12], P('fsdp')
- vectors_new: float32 [1024, 12], P('fsdp')
- vectors_half: bfloat16 [1024, 12], P('fsdp')
Inputs may be any that keep to these rules, and one draw needn't show every extreme that they name: `crop_counts`: per device, entry 0 counts crops of 50 tokens (res group 0) or of 145 tokens (res group 1) and is 1 or more; entry 1 counts crops of 10 tokens in group 0 and is 0 in group 1. Crops fill the device's rows from the first one on, longer kind first, and fit in its 256 rows; the rows after them are padding.
All inputs are finite; a program needn't handle non-finite values.
Results may differ from a plain program's by a relative error of at most 0.014.
The roundings to bfloat16 on the way count: a program that leaves them out, or rounds other values in their place, can miss the bound.
Values may be sent and summed in bfloat16 or wider, within the bound.
No kernel may reach another device: no remote copies, remote signals or barrier semaphores. Data moves between devices by JAX's collectives and lax.ppermute only.
A program may use at most 320 MiB of HBM per device.

v0:
```python
from functools import partial

import jax
import jax.numpy as jnp
from jax import lax
from jax.sharding import PartitionSpec as P

D = 1024
HEADS = 16
HEAD = 64
FF = 4096
GLOBAL_LEN = 50
LOCAL_LEN = 10
IMAGE_LEN = 145
STEP = 3


EPS_NORM = 1e-06
EPS_SQUARE = 1e-30
EPS_WEIGHT = 1e-06
RATE = 0.4
padding_label = 1000000
MASKED = -1e30
query_rows = 512


def norm_forward(values, gain, shift):
    mean = jnp.mean(values, axis=-1, keepdims=True)
    centred = values - mean
    variance = jnp.mean(centred * centred, axis=-1, keepdims=True)
    return centred * lax.rsqrt(variance + EPS_NORM) * gain + shift


def segment_ids(counts, group, rows):
    first_len = jnp.where(group == 0, GLOBAL_LEN, IMAGE_LEN).astype(jnp.int32)
    first_count = counts[0]
    second_count = counts[1]
    position = jnp.arange(rows, dtype=jnp.int32)
    first_end = first_len * first_count
    second_end = first_end + LOCAL_LEN * second_count
    later = first_count + (position - first_end) // LOCAL_LEN
    label = jnp.where(
        position < first_end,
        position // first_len,
        jnp.where(position < second_end, later, padding_label),
    )
    return label


def unpack(vectors):
    ratio = FF // D
    up_bias = vectors[:, 3 : 3 + ratio].T.reshape(FF)
    base = 4 + ratio
    return (
        vectors[:, 0],
        vectors[:, 1],
        vectors[:, 2],
        up_bias,
        vectors[:, 3 + ratio],
        vectors[:, base],
        vectors[:, base + 1],
        vectors[:, base + 2],
        vectors[:, base + 3],
    )


def attend_forward(query_block, segment_block, keys, values, segment, scale):
    scores = (
        jnp.einsum("qhd,khd->hqk", query_block, keys, preferred_element_type=jnp.float32) * scale
    )
    allowed = segment_block[:, None] == segment[None, :]
    scores = jnp.where(allowed[None], scores, MASKED)
    top = jnp.max(scores, axis=2, keepdims=True)
    weights = jnp.exp(scores - top)
    total = jnp.sum(weights, axis=2, keepdims=True)
    probs = (weights / total).astype(jnp.bfloat16)
    mixed = jnp.einsum("hqk,khd->qhd", probs, values, preferred_element_type=jnp.float32)
    return (mixed.astype(jnp.bfloat16), (top + jnp.log(total))[:, :, 0])


def attend_backward(
    query_block, segment_block, grad_block, logsum_block, keys, values, segment, scale
):
    scores = (
        jnp.einsum("qhd,khd->hqk", query_block, keys, preferred_element_type=jnp.float32) * scale
    )
    allowed = segment_block[:, None] == segment[None, :]
    scores = jnp.where(allowed[None], scores, MASKED)
    probs = jnp.exp(scores - logsum_block[:, :, None])
    grad_probs = jnp.einsum("qhd,khd->hqk", grad_block, values, preferred_element_type=jnp.float32)
    inner = jnp.sum(probs * grad_probs, axis=2, keepdims=True)
    grad_scores = (probs * (grad_probs - inner)).astype(jnp.bfloat16)
    grad_query = (
        jnp.einsum("hqk,khd->qhd", grad_scores, keys, preferred_element_type=jnp.float32) * scale
    )
    grad_keys = (
        jnp.einsum("hqk,qhd->khd", grad_scores, query_block, preferred_element_type=jnp.float32)
        * scale
    )
    grad_values = jnp.einsum(
        "hqk,qhd->khd", probs.astype(jnp.bfloat16), grad_block, preferred_element_type=jnp.float32
    )
    return (grad_query, grad_keys, grad_values)


def split_heads(projected, rows):
    queries = projected[:, :D].reshape(rows, HEADS, HEAD)
    keys = projected[:, D : 2 * D].reshape(rows, HEADS, HEAD)
    values = projected[:, 2 * D :].reshape(rows, HEADS, HEAD)
    return (queries, keys, values)


def forward(tokens, segment, weights):
    weight_qkv, weight_out, weight_up, weight_down, vector_half = weights
    (
        query_bias,
        value_bias,
        out_bias,
        up_bias,
        down_bias,
        gain_one,
        shift_one,
        gain_two,
        shift_two,
    ) = unpack(vector_half.astype(jnp.float32))
    rows = tokens.shape[0]
    scale = HEAD ** (-0.5)
    normed = norm_forward(tokens, gain_one, shift_one).astype(jnp.bfloat16)
    bias_qkv = jnp.concatenate([query_bias, jnp.zeros_like(query_bias), value_bias])
    projected = (jnp.dot(normed, weight_qkv, preferred_element_type=jnp.float32) + bias_qkv).astype(
        jnp.bfloat16
    )
    queries, keys, values = split_heads(projected, rows)
    block = min(rows, query_rows)
    count = rows // block

    def forward_one_block(pair):
        return attend_forward(pair[0], pair[1], keys, values, segment, scale)

    mixed, logsum = lax.map(
        forward_one_block,
        (queries.reshape(count, block, HEADS, HEAD), segment.reshape(count, block)),
    )
    mixed = mixed.reshape(rows, D)
    branch = jnp.dot(mixed, weight_out, preferred_element_type=jnp.float32) + out_bias
    middle = tokens + branch
    normed_two = norm_forward(middle, gain_two, shift_two).astype(jnp.bfloat16)
    before = jnp.dot(normed_two, weight_up, preferred_element_type=jnp.float32) + up_bias
    hidden = jax.nn.gelu(before, approximate=False).astype(jnp.bfloat16)
    second = jnp.dot(hidden, weight_down, preferred_element_type=jnp.float32) + down_bias
    output = middle + second
    return (output, (normed, projected, mixed, logsum, middle, normed_two, before, hidden))


def backward(tokens, segment, weights, saved, grad_output):
    weight_qkv, weight_out, weight_up, weight_down, vector_half = weights
    (
        query_bias,
        value_bias,
        out_bias,
        up_bias,
        down_bias,
        gain_one,
        shift_one,
        gain_two,
        shift_two,
    ) = unpack(vector_half.astype(jnp.float32))
    normed, projected, mixed, logsum, middle, normed_two, before, hidden = saved
    rows = tokens.shape[0]
    scale = HEAD ** (-0.5)
    grad_second = grad_output.astype(jnp.bfloat16)
    grad_down = jnp.einsum("tf,td->fd", hidden, grad_second, preferred_element_type=jnp.float32)
    grad_down_bias = jnp.sum(grad_second.astype(jnp.float32), axis=0)
    grad_hidden = jnp.einsum(
        "td,fd->tf", grad_second, weight_down, preferred_element_type=jnp.float32
    )
    _, gelu_back = jax.vjp(partial(jax.nn.gelu, approximate=False), before)
    grad_before = gelu_back(grad_hidden)[0].astype(jnp.bfloat16)
    grad_up = jnp.einsum("td,tf->df", normed_two, grad_before, preferred_element_type=jnp.float32)
    grad_up_bias = jnp.sum(grad_before.astype(jnp.float32), axis=0)
    grad_normed_two = jnp.einsum(
        "tf,df->td", grad_before, weight_up, preferred_element_type=jnp.float32
    )
    _, norm_back_two = jax.vjp(norm_forward, middle, gain_two, shift_two)
    grad_middle_part, grad_gain_two, grad_shift_two = norm_back_two(grad_normed_two)
    grad_middle = grad_output + grad_middle_part
    grad_branch = grad_middle.astype(jnp.bfloat16)
    grad_weight_out = jnp.einsum(
        "td,te->de", mixed, grad_branch, preferred_element_type=jnp.float32
    )
    grad_out_bias = jnp.sum(grad_branch.astype(jnp.float32), axis=0)
    grad_mixed = jnp.einsum(
        "te,de->td", grad_branch, weight_out, preferred_element_type=jnp.float32
    ).astype(jnp.bfloat16)
    queries, keys, values = split_heads(projected, rows)
    block = min(rows, query_rows)
    count = rows // block

    def backward_one_block(items):
        return attend_backward(items[0], items[1], items[2], items[3], keys, values, segment, scale)

    grad_query, grad_keys, grad_values = lax.map(
        backward_one_block,
        (
            queries.reshape(count, block, HEADS, HEAD),
            segment.reshape(count, block),
            grad_mixed.reshape(count, block, HEADS, HEAD),
            logsum,
        ),
    )
    grad_projected = jnp.concatenate(
        [
            grad_query.reshape(rows, D),
            jnp.sum(grad_keys, axis=0).reshape(rows, D),
            jnp.sum(grad_values, axis=0).reshape(rows, D),
        ],
        axis=1,
    ).astype(jnp.bfloat16)
    grad_weight_qkv = jnp.einsum(
        "td,te->de", normed, grad_projected, preferred_element_type=jnp.float32
    )
    grad_bias_qkv = jnp.sum(grad_projected.astype(jnp.float32), axis=0)
    grad_normed = jnp.einsum(
        "te,de->td", grad_projected, weight_qkv, preferred_element_type=jnp.float32
    )
    _, norm_back_one = jax.vjp(norm_forward, tokens, gain_one, shift_one)
    grad_tokens_part, grad_gain_one, grad_shift_one = norm_back_one(grad_normed)
    grad_tokens = grad_middle + grad_tokens_part
    up_columns = grad_up_bias.reshape(FF // D, D).T
    grad_vectors = jnp.concatenate(
        [
            grad_bias_qkv[:D, None],
            grad_bias_qkv[2 * D :, None],
            grad_out_bias[:, None],
            up_columns,
            grad_down_bias[:, None],
            grad_gain_one[:, None],
            grad_shift_one[:, None],
            grad_gain_two[:, None],
            grad_shift_two[:, None],
        ],
        axis=1,
    )
    return (grad_tokens, (grad_weight_qkv, grad_weight_out, grad_up, grad_down, grad_vectors))


def on_device(
    tokens_in,
    cotangent,
    crop_counts,
    group_tokens,
    weight_qkv,
    rows_qkv,
    cols_qkv,
    weight_out,
    rows_out,
    cols_out,
    weight_up,
    rows_up,
    cols_up,
    weight_down,
    rows_down,
    cols_down,
    vectors,
    moment_vec,
):
    group = lax.axis_index("res")
    rows = tokens_in.shape[0]
    segment = segment_ids(crop_counts.reshape(2), group, rows)
    valid = (segment < padding_label).astype(jnp.float32)
    tokens = tokens_in.astype(jnp.float32)
    gathered = (
        lax.all_gather(weight_qkv.astype(jnp.bfloat16), "fsdp", axis=0, tiled=True),
        lax.all_gather(weight_out.astype(jnp.bfloat16), "fsdp", axis=0, tiled=True),
        lax.all_gather(weight_up.astype(jnp.bfloat16), "fsdp", axis=0, tiled=True),
        lax.all_gather(weight_down.astype(jnp.bfloat16), "fsdp", axis=0, tiled=True),
        lax.all_gather(vectors.astype(jnp.bfloat16), "fsdp", axis=0, tiled=True),
    )
    output, saved = forward(tokens, segment, gathered)
    grad_output = cotangent.astype(jnp.float32) * valid[:, None]
    used = (
        lax.all_gather(weight_qkv.astype(jnp.bfloat16), "fsdp", axis=0, tiled=True),
        lax.all_gather(weight_out.astype(jnp.bfloat16), "fsdp", axis=0, tiled=True),
        lax.all_gather(weight_up.astype(jnp.bfloat16), "fsdp", axis=0, tiled=True),
        lax.all_gather(weight_down.astype(jnp.bfloat16), "fsdp", axis=0, tiled=True),
        lax.all_gather(vectors.astype(jnp.bfloat16), "fsdp", axis=0, tiled=True),
    )
    kept = forward(tokens, segment, used)[1]
    grad_tokens, local_grads = backward(tokens, segment, used, kept, grad_output)
    total = (group_tokens[0] + group_tokens[1]).astype(jnp.float32)
    share = jnp.where(group == 0, group_tokens[0], group_tokens[1]).astype(jnp.float32) / total
    weighted = [share * grad for grad in local_grads]
    masters = (weight_qkv, weight_out, weight_up, weight_down, vectors)
    fsdp_count = lax.axis_size("fsdp")
    shards = (
        lax.psum_scatter(weighted[0], "fsdp", scatter_dimension=0, tiled=True),
        lax.psum_scatter(weighted[1], "fsdp", scatter_dimension=0, tiled=True),
        lax.psum_scatter(weighted[2], "fsdp", scatter_dimension=0, tiled=True),
        lax.psum_scatter(weighted[3], "fsdp", scatter_dimension=0, tiled=True),
        lax.psum_scatter(weighted[4], "fsdp", scatter_dimension=0, tiled=True),
    )
    shards = lax.psum((shards[0], shards[1], shards[2], shards[3], shards[4]), ("res", "dp"))
    reduced = [shards[index] for index in range(5)]
    decay = 1.0 - float(STEP) ** (-0.8)
    row_stats = (rows_qkv, rows_out, rows_up, rows_down)
    col_stats = (cols_qkv, cols_out, cols_up, cols_down)
    squares = [reduced[index] * reduced[index] + EPS_SQUARE for index in range(4)]
    rows_new = [
        decay * row_stats[index] + (1.0 - decay) * jnp.mean(squares[index], axis=1)
        for index in range(4)
    ]
    stats = lax.psum(
        (
            jnp.sum(squares[0], axis=0),
            jnp.sum(squares[1], axis=0),
            jnp.sum(squares[2], axis=0),
            jnp.sum(squares[3], axis=0),
            jnp.stack([jnp.sum(entry) for entry in rows_new]),
            jnp.stack([jnp.sum(masters[index] * masters[index]) for index in range(4)]),
            jnp.sum(vectors * vectors, axis=0),
        ),
        "fsdp",
    )
    results = []
    for index in range(4):
        weight = masters[index]
        full_rows = weight.shape[0] * fsdp_count
        cols_new = decay * col_stats[index] + (1.0 - decay) * stats[index] / full_rows
        row_mean = stats[4][index] / full_rows
        scale = jnp.sqrt(stats[5][index] / (full_rows * weight.shape[1]) + EPS_WEIGHT)
        estimate = rows_new[index][:, None] * cols_new[None, :] / row_mean
        weight_new = weight - RATE * scale * reduced[index] * lax.rsqrt(estimate)
        results.extend(
            [reduced[index], rows_new[index], cols_new, weight_new, weight_new.astype(jnp.bfloat16)]
        )
    grad_vec = reduced[4]
    moment_new = decay * moment_vec + (1.0 - decay) * (grad_vec * grad_vec + EPS_SQUARE)
    vector_scale = jnp.sqrt(stats[6] / D + EPS_WEIGHT)
    vectors_new = vectors - RATE * vector_scale[None, :] * grad_vec * lax.rsqrt(moment_new)
    return tuple(
        [output.astype(jnp.bfloat16), grad_tokens]
        + results
        + [grad_vec, moment_new, vectors_new, vectors_new.astype(jnp.bfloat16)]
    )


def solution(mesh):
    return jax.shard_map(
        on_device,
        mesh=mesh,
        in_specs=(
            P(("res", "dp", "fsdp"), None),
            P(("res", "dp", "fsdp"), None),
            P("res", "dp", "fsdp", None),
            P(),
            P("fsdp", None),
            P("fsdp"),
            P(),
            P("fsdp", None),
            P("fsdp"),
            P(),
            P("fsdp", None),
            P("fsdp"),
            P(),
            P("fsdp", None),
            P("fsdp"),
            P(),
            P("fsdp", None),
            P("fsdp", None),
        ),
        out_specs=(
            P(("res", "dp", "fsdp"), None),
            P(("res", "dp", "fsdp"), None),
            P("fsdp", None),
            P("fsdp"),
            P(),
            P("fsdp", None),
            P("fsdp", None),
            P("fsdp", None),
            P("fsdp"),
            P(),
            P("fsdp", None),
            P("fsdp", None),
            P("fsdp", None),
            P("fsdp"),
            P(),
            P("fsdp", None),
            P("fsdp", None),
            P("fsdp", None),
            P("fsdp"),
            P(),
            P("fsdp", None),
            P("fsdp", None),
            P("fsdp", None),
            P("fsdp", None),
            P("fsdp", None),
            P("fsdp", None),
        ),
        check_vma=False,
    )
```

profile of v0, /device:TPU:0, one launch (start us, length us, event | category | flops | bytes accessed | tf_op | source)
XLA Modules:
  0.0 1496.0 jit_solution(8950766783842660658)
XLA Ops:
  7.3 8.6 multiply_reduce_fusion.2
  18.0 10.7 multiply_reduce_fusion.1
  28.8 11.9 multiply_reduce_fusion
  45.9 5.4 all_gather.20
  53.5 46.0 %all-gather.5.cloned.1.call-done = bf16[1024,3072]{1,0:T(8,128)(2,1)} async-done(((bf16[512,3072]{1,0:T(8,128)(2,1)}), bf16[1024,3072]{1,0:T(8,128)(2,1)}) %all-gather.5.cloned.1.call-update) | async-done | bytes 6291472 | tf_op jit(solution)/shard_map/all_gather | solution.py:273
  99.4 4.7 fusion.12
  108.7 26.0 %all-gather.7.cloned.1.call-done = bf16[1024,1024]{1,0:T(8,128)(2,1)} async-done(((bf16[512,1024]{1,0:T(8,128)(2,1)}), bf16[1024,1024]{1,0:T(8,128)(2,1)}) %all-gather.7.cloned.1.call-update) | async-done | bytes 2097168 | tf_op jit(solution)/shard_map/all_gather | solution.py:274
  137.4 103.5 %all-gather.9.cloned.1.call-done = bf16[1024,4096]{1,0:T(8,128)(2,1)} async-done(((bf16[512,4096]{1,0:T(8,128)(2,1)}), bf16[1024,4096]{1,0:T(8,128)(2,1)}) %all-gather.9.cloned.1.call-update) | async-done | bytes 8388624 | tf_op jit(solution)/shard_map/all_gather | solution.py:275
  240.9 16.5 %multiply_convert_fusion.1 = (bf16[256,4096]{1,0:T(8,128)(2,1)}, f32[256,4096]{1,0:T(8,128)}, f32[256,4096]{1,0:T(8,128)}) fusion(f32[4096]{0:T(1024)S(1)} %bitcast.128, bf16[1024,4096]{1,0:T(8,128)(2,1)} %all-gather.9.cloned.1.call-done, f32[256,1024]{1,0:T(8,128)S(1)} %get-tuple-element.196, f32[1024]{0:T(1024)S(1)} %bitcast.119, f32[1024]{0:T(1024)S(1)} %bitcast.115, ...), kind=kOutput, calls=%fused_computation.26 | convolution fusion | flops 2218000384 | bytes 19949568 | tf_op jit(solution)/shard_map/dot_general | solution.py:148
  257.4 89.5 %all-gather.11.cloned.1.call-done = bf16[4096,1024]{1,0:T(8,128)(2,1)} async-done(((bf16[2048,1024]{1,0:T(8,128)(2,1)}), bf16[4096,1024]{1,0:T(8,128)(2,1)}) %all-gather.11.cloned.1.call-update) | async-done | bytes 8388624 | tf_op jit(solution)/shard_map/all_gather | solution.py:276
  346.9 11.7 convert_reduce_fusion
  371.1 4.1 multiply_reduce_fusion.3
  378.4 6.6 convolution_multiply_fusion.2
  385.3 10.0 convolution_multiply_fusion.1
  395.4 9.8 convolution_multiply_fusion
  407.0 5.2 fusion.53
  414.5 5.6 reduce-scatter.8.cloned.1.call-done
  420.1 146.8 %reduce-scatter.6.cloned.1.call-done = f32[512,3072]{1,0:T(8,128)} async-done(((f32[1024,3072]{1,0:T(8,128)}), f32[512,3072]{1,0:T(8,128)}) %reduce-scatter.6.cloned.1.call-update) | async-done | bytes 6291472 | tf_op jit(solution)/shard_map/reduce_scatter | solution.py:296
  566.9 191.6 %reduce-scatter.10.cloned.1.call-done = f32[512,4096]{1,0:T(8,128)} async-done(((f32[1024,4096]{1,0:T(8,128)}), f32[512,4096]{1,0:T(8,128)}) %reduce-scatter.10.cloned.1.call-update) | async-done | bytes 8388624 | tf_op jit(solution)/shard_map/reduce_scatter | solution.py:298
  758.4 191.4 %reduce-scatter.12.cloned.1.call-done = f32[2048,1024]{1,0:T(8,128)} async-done(((f32[4096,1024]{1,0:T(8,128)}), f32[2048,1024]{1,0:T(8,128)}) %reduce-scatter.12.cloned.1.call-update) | async-done | bytes 8388624 | tf_op jit(solution)/shard_map/reduce_scatter | solution.py:299
  955.4 6.6 fusion.26
  962.6 64.3 %psum.94 = f32[512,12]{0,1:T(8,128)S(1)} all-reduce(f32[512,12]{0,1:T(8,128)} %reduce-scatter.14.cloned.1.call-done), channel_id=1, replica_groups=mesh['res'=2,'dp'=8,'fsdp'=2] {'res','dp'}, use_global_device_ids=true, to_apply=%region_50.51 | all-reduce | flops 6144 | bytes 49152 | tf_op jit(solution)/shard_map/psum | solution.py:302
  1026.9 385.2 %all-reduce.4.cloned.1.call-done = (f32[512,3072]{1,0:T(8,128)}, f32[2048,1024]{1,0:T(8,128)}, f32[512,4096]{1,0:T(8,128)}, f32[512,1024]{1,0:T(8,128)}) async-done(((f32[512,3072]{1,0:T(8,128)}, f32[2048,1024]{1,0:T(8,128)}, f32[512,4096]{1,0:T(8,128)}, f32[512,1024]{1,0:T(8,128)}), (f32[512,3072]{1,0:T(8,128)}, f32[2048,1024]{1,0:T(8,128)}, f32[512,4096]{1,0:T(8,128)}, ...) | async-done | bytes 25165840 | tf_op jit(solution)/shard_map/psum | solution.py:302
  1414.2 5.0 fusion.2
  1428.3 8.5 all-reduce.1
  1444.2 3.8 fusion.58
  1448.0 8.7 fusion.59
  1458.4 8.2 fusion.57
  1466.6 7.8 fusion.56
  1474.4 6.2 copy.75
  1481.9 3.4 copy.77
  1485.3 3.4 copy.78
  (194 shorter events, 54.9 us)
Async XLA Ops:
  7.2 92.2 %all-gather.5.cloned.1.call-start = ((), (), s32[]{:S(2)}) async-start(), calls=%async_computation.5 | async-start | bytes 9437184 | tf_op jit(solution)/shard_map/all_gather | solution.py:273
  15.9 118.9 %all-gather.7.cloned.1.call-start = ((), (), s32[]{:S(2)}) async-start(), calls=%async_computation.6 | async-start | bytes 3145728 | tf_op jit(solution)/shard_map/all_gather | solution.py:274
  18.0 222.9 %all-gather.9.cloned.1.call-start = ((), (), s32[]{:S(2)}) async-start(), calls=%async_computation.7 | async-start | bytes 12582912 | tf_op jit(solution)/shard_map/all_gather | solution.py:275
  28.8 318.1 %all-gather.11.cloned.1.call-start = ((), (), s32[]{:S(2)}) async-start(), calls=%async_computation.8 | async-start | bytes 12582912 | tf_op jit(solution)/shard_map/all_gather | solution.py:276
  40.7 12.2 copy-start.3
  40.7 379.4 %reduce-scatter.8.cloned.1.call-start = ((), (), s32[]{:S(2)}) async-start(), calls=%async_computation.10 | async-start | bytes 6291456 | tf_op jit(solution)/shard_map/reduce_scatter | solution.py:297
  108.7 148.7 %copy-start.17 = (bf16[16,64,256]{2,1,0:T(8,128)(2,1)}, bf16[16,64,256]{2,1,0:T(8,128)(2,1)S(1)}, u32[]{:S(2)}) copy-start(bf16[16,64,256]{2,1,0:T(8,128)(2,1)S(1)} %fusion.32) | copy-start | bytes 1572868
  240.9 106.0 %copy-start.10 = (bf16[256,1024]{1,0:T(8,128)(2,1)S(1)}, bf16[256,1024]{1,0:T(8,128)(2,1)}, u32[]{:S(2)}) copy-start(bf16[256,1024]{1,0:T(8,128)(2,1)} %param.19) | copy-start | bytes 1572868
  346.9 11.7 copy-start.45
  365.7 201.2 %reduce-scatter.6.cloned.1.call-start = ((), (), s32[]{:S(2)}) async-start(), calls=%async_computation.9 | async-start | bytes 18874368 | tf_op jit(solution)/shard_map/reduce_scatter | solution.py:296
  385.0 373.4 %reduce-scatter.10.cloned.1.call-start = ((), (), s32[]{:S(2)}) async-start(), calls=%async_computation.11 | async-start | bytes 25165824 | tf_op jit(solution)/shard_map/reduce_scatter | solution.py:298
  395.3 554.6 %reduce-scatter.12.cloned.1.call-start = ((), (), s32[]{:S(2)}) async-start(), calls=%async_computation.12 | async-start | bytes 25165824 | tf_op jit(solution)/shard_map/reduce_scatter | solution.py:299
  405.2 557.4 %reduce-scatter.14.cloned.1.call-start = ((), (), s32[]{:S(2)}) async-start(), calls=%async_computation.13 | async-start | bytes 98304 | tf_op jit(solution)/shard_map/reduce_scatter | solution.py:300
  414.4 997.6 %all-reduce.4.cloned.1.call-start = ((), (), s32[]{:S(2)}) async-start(), calls=%async_computation.14 | async-start | bytes 50331648 | tf_op jit(solution)/shard_map/psum | solution.py:302
  1026.9 416.6 %copy-start.25 = (f32[512,12]{0,1:T(8,128)}, f32[512,12]{0,1:T(8,128)S(1)}, u32[]{:S(2)}) copy-start(f32[512,12]{0,1:T(8,128)S(1)} %psum.94) | copy-start | bytes 73732
  1420.8 21.9 %copy-start.33 = (f32[3072]{0:T(1024)S(1)}, f32[3072]{0:T(1024)}, u32[]{:S(2)}) copy-start(f32[3072]{0:T(1024)} %param.24) | copy-start | bytes 36868
  1420.8 22.6 %copy-start.38 = (f32[1024]{0:T(1024)S(1)}, f32[1024]{0:T(1024)}, u32[]{:S(2)}) copy-start(f32[1024]{0:T(1024)} %param.27) | copy-start | bytes 12292
  1420.8 22.6 %copy-start.39 = (f32[1024]{0:T(1024)S(1)}, f32[1024]{0:T(1024)}, u32[]{:S(2)}) copy-start(f32[1024]{0:T(1024)} %param.33) | copy-start | bytes 12292
  1420.8 22.6 %copy-start.31 = (f32[4096]{0:T(1024)S(1)}, f32[4096]{0:T(1024)}, u32[]{:S(2)}) copy-start(f32[4096]{0:T(1024)} %param.30) | copy-start | bytes 49156
  1420.8 22.7 %copy-start.28 = (f32[512,12]{0,1:T(8,128)S(1)}, f32[512,12]{0,1:T(8,128)}, u32[]{:S(2)}) copy-start(f32[512,12]{0,1:T(8,128)} %param.35) | copy-start | bytes 73732
  1420.8 23.4 %copy-start.4 = (f32[512,1024]{1,0:T(8,128)S(1)}, f32[512,1024]{1,0:T(8,128)}, u32[]{:S(2)}) copy-start(f32[512,1024]{1,0:T(8,128)} %get-tuple-element.213) | copy-start | bytes 6291460
  1424.4 42.2 %copy-start.29 = (f32[2048]{0:T(1024)}, f32[2048]{0:T(1024)S(1)}, u32[]{:S(2)}) copy-start(f32[2048]{0:T(1024)S(1)} %get-tuple-element.224) | copy-start | bytes 24580
  1425.0 31.7 %copy-start.34 = (f32[512]{0:T(512)}, f32[512]{0:T(512)S(1)}, u32[]{:S(2)}) copy-start(f32[512]{0:T(512)S(1)} %get-tuple-element.219) | copy-start | bytes 6148
  1425.6 31.0 %copy-start.35 = (f32[512]{0:T(512)}, f32[512]{0:T(512)S(1)}, u32[]{:S(2)}) copy-start(f32[512]{0:T(512)S(1)} %get-tuple-element.209) | copy-start | bytes 6148
  1425.6 31.0 %copy-start.37 = (f32[512]{0:T(512)}, f32[512]{0:T(512)S(1)}, u32[]{:S(2)}) copy-start(f32[512]{0:T(512)S(1)} %get-tuple-element.214) | copy-start | bytes 6148
  1442.7 14.0 copy-start.27
  1443.4 13.3 copy-start.30
  1443.4 23.1 %copy-start.32 = (f32[1024]{0:T(1024)}, f32[1024]{0:T(1024)S(1)}, u32[]{:S(2)}) copy-start(f32[1024]{0:T(1024)S(1)} %multiply_add_fusion.8) | copy-start | bytes 12292
  1443.5 13.2 copy-start.26
  1448.0 8.8 slice-start.4
  1448.0 10.4 slice-start.5
  1456.7 9.9 slice-start
  (30 other events, 99.0 us)
Sparse Core Ops, SparseCore 0:
  16.0 83.4 all-gather.4
  101.6 33.1 all-gather.6
  136.8 103.9 all-gather.8
  242.9 103.9 all-gather.10
  365.8 54.2 reduce-scatter.7
  422.4 144.4 reduce-scatter.5
  569.3 189.1 reduce-scatter.9
  760.7 189.0 reduce-scatter.11
  952.7 9.8 reduce-scatter.13
  968.1 443.8 all-reduce.3
where the time goes:
time: 1510 us; the launch traced here: 1500 us
  waiting for transfers between devices  1190 us (79%)
  other arithmetic  90.5 us (6%)
  matrix products  89.8 us (6%)
  blocking collectives  78.1 us (5%)
  local copies, waits for them, and re-layouts  25.9 us (2%)
  between operations  24.7 us (2%)
    psum x1, waiting for transfers between devices, on_device(): lax.psum((shards[0], shards[1], shards[2], shards[3], shards[4]), ('res',...  385 us
    reduce_scatter x1, waiting for transfers between devices, on_device(): lax.psum_scatter(weighted[2], 'fsdp', scatter_dimension=0, tiled=True)  192 us
    reduce_scatter x1, waiting for transfers between devices, on_device(): lax.psum_scatter(weighted[3], 'fsdp', scatter_dimension=0, tiled=True)  191 us
    reduce_scatter x1, waiting for transfers between devices, on_device(): lax.psum_scatter(weighted[0], 'fsdp', scatter_dimension=0, tiled=True)  147 us
    all_gather x1, waiting for transfers between devices, on_device(): lax.all_gather(weight_up.astype(jnp.bfloat16), 'fsdp', axis=0, tiled=True)  103 us
    all_gather x1, waiting for transfers between devices, on_device(): lax.all_gather(weight_down.astype(jnp.bfloat16), 'fsdp', axis=0, tiled=True)  89.5 us
    psum x1, blocking collectives, on_device(): lax.psum((shards[0], shards[1], shards[2], shards[3], shards[4]), ('res',...  64.3 us
    all_gather x1, waiting for transfers between devices, on_device(): lax.all_gather(weight_qkv.astype(jnp.bfloat16), 'fsdp', axis=0, tiled=True)  46 us
  transfers between devices with their start and end apart: 10, of which 10 were waited for; matrix products, arithmetic and copies ran while one was open for 8% of the time, Pallas kernels for 0%

commit v1 on v0

v1 whole, which is shorter than its diff:
```python
from functools import partial

import jax
import jax.numpy as jnp
from jax import lax
from jax.experimental import pallas as pl
from jax.experimental.pallas import tpu as pltpu
from jax.sharding import PartitionSpec as P

D = 1024
HEADS = 16
HEAD = 64
FF = 4096
GLOBAL_LEN = 50
LOCAL_LEN = 10
IMAGE_LEN = 145
STEP = 3

EPS_NORM = 1e-06
EPS_SQUARE = 1e-30
EPS_WEIGHT = 1e-06
RATE = 0.4
padding_label = 1000000
MASKED = -1e30
DECAY = 1.0 - float(STEP) ** (-0.8)

bf16 = jnp.bfloat16
f32 = jnp.float32


def norm_forward(values, gain, shift):
    mean = jnp.mean(values, axis=-1, keepdims=True)
    centred = values - mean
    variance = jnp.mean(centred * centred, axis=-1, keepdims=True)
    return centred * lax.rsqrt(variance + EPS_NORM) * gain + shift


def segment_ids(counts, group, rows):
    first_len = jnp.where(group == 0, GLOBAL_LEN, IMAGE_LEN).astype(jnp.int32)
    first_count = counts[0]
    second_count = counts[1]
    position = jnp.arange(rows, dtype=jnp.int32)
    first_end = first_len * first_count
    second_end = first_end + LOCAL_LEN * second_count
    later = first_count + (position - first_end) // LOCAL_LEN
    return jnp.where(
        position < first_end,
        position // first_len,
        jnp.where(position < second_end, later, padding_label),
    )


def unpack(vectors):
    ratio = FF // D
    up_bias = vectors[:, 3 : 3 + ratio].T.reshape(FF)
    base = 4 + ratio
    return (
        vectors[:, 0],
        vectors[:, 1],
        vectors[:, 2],
        up_bias,
        vectors[:, 3 + ratio],
        vectors[:, base],
        vectors[:, base + 1],
        vectors[:, base + 2],
        vectors[:, base + 3],
    )


def dot(a, b):
    return jnp.dot(a, b, preferred_element_type=f32)


def dot_nt(a, b):
    return lax.dot_general(a, b, (((1,), (1,)), ((), ())), preferred_element_type=f32)


def dot_tn(a, b):
    return lax.dot_general(a, b, (((0,), (0,)), ((), ())), preferred_element_type=f32)


def head_probs(queries, keys, allowed):
    scores = dot_nt(queries, keys) * HEAD ** (-0.5)
    scores = jnp.where(allowed, scores, MASKED)
    weights = jnp.exp(scores - jnp.max(scores, axis=1, keepdims=True))
    return weights * (1.0 / jnp.sum(weights, axis=1, keepdims=True))


def attend_kernel(seg_col, seg_row, projected, mixed):
    allowed = seg_col[...] == seg_row[...]
    lane = lax.broadcasted_iota(jnp.int32, (projected.shape[0], 2 * HEAD), 1)
    first = lane < HEAD
    for pair in range(HEADS // 2):
        queries, keys, values = (
            projected[:, at : at + 2 * HEAD]
            for at in range(2 * HEAD * pair, 3 * D, D)
        )
        parts = []
        for mask in (first, jnp.logical_not(first)):
            probs = head_probs(jnp.where(mask, queries, 0), keys, allowed)
            parts.append(dot(probs.astype(bf16), values))
        at = 2 * HEAD * pair
        mixed[:, at : at + 2 * HEAD] = jnp.where(first, *parts).astype(bf16)


def attend_back_kernel(seg_col, seg_row, projected, grad_mixed, grad):
    allowed = seg_col[...] == seg_row[...]
    lane = lax.broadcasted_iota(jnp.int32, (projected.shape[0], 2 * HEAD), 1)
    first = lane < HEAD
    scale = HEAD ** (-0.5)
    for pair in range(HEADS // 2):
        at = 2 * HEAD * pair
        queries, keys, values = (
            projected[:, start : start + 2 * HEAD] for start in range(at, 3 * D, D)
        )
        out = grad_mixed[:, at : at + 2 * HEAD]
        parts = []
        for mask in (first, jnp.logical_not(first)):
            probs = head_probs(jnp.where(mask, queries, 0), keys, allowed)
            grad_probs = dot_nt(jnp.where(mask, out, 0), values)
            inner = jnp.sum(probs * grad_probs, axis=1, keepdims=True)
            grad_scores = (probs * (grad_probs - inner)).astype(bf16)
            parts.append(
                (
                    dot(grad_scores, keys) * scale,
                    dot_tn(grad_scores, queries) * scale,
                    dot_tn(probs.astype(bf16), out),
                )
            )
        for index in range(3):
            both = jnp.where(first, parts[0][index], parts[1][index])
            grad[:, index * D + at : index * D + at + 2 * HEAD] = both.astype(bf16)


def attend(segment, projected):
    shape = (projected.shape[0], D)
    values = [segment[:, None], segment[None, :], projected]
    return call("attend", attend_kernel, [(shape, bf16)], [], values, [])[0]


def attend_back(segment, projected, grad_mixed):
    values = [segment[:, None], segment[None, :], projected, grad_mixed]
    return call("attend_back", attend_back_kernel, [(projected.shape, bf16)], [], values, [])[0]


SWAP = ((0, 1), (1, 0))
BLOCK = 256
UNIT = 512


def in_hbm(value):
    return pltpu.with_memory_space_constraint(value, pltpu.HBM)


def in_vmem(value):
    return pltpu.with_memory_space_constraint(value, pltpu.VMEM)


def any_spec():
    return pl.BlockSpec(memory_space=pl.ANY)


def gelu_parts(before):
    normal = 0.5 * (1.0 + lax.erf(before * (0.5**0.5)))
    slope = normal + before * jnp.exp(-0.5 * before * before) * ((2.0 * jnp.pi) ** -0.5)
    return (before * normal).astype(bf16), slope


def forward_matmul(finish, where, act, weight, pieces, extras, out_types, deps):
    rows, own_rows = act.shape[0], weight.shape[0]
    cols = weight.shape[1]
    blocks = cols // UNIT
    share = blocks // len(pieces)
    half_rows = pieces[0][0].shape[0]
    flat = [piece for pair in pieces for piece in pair]
    count = len(extras)

    def kernel(where, act, weight, *refs):
        pairs, refs = refs[: len(flat)], refs[len(flat) :]
        outs, (squares, rest, total) = refs[count + len(deps) : -3], refs[-3:]
        step = pl.program_id(0)
        quarter = own_rows // 4
        y, first = where[0], where[1]

        @pl.when(step == 0)
        def _():
            for k in range(4):
                at = pl.multiple_of((1 - y) * own_rows + (first ^ k) * quarter, 128)
                rest[:, k * quarter : (k + 1) * quarter] = act[:, pl.ds(at, quarter)]

        value = weight[...]
        squares[...] = jnp.sum((value * value).reshape(-1, 8, value.shape[1]), axis=0)
        own = act[:, pl.ds(pl.multiple_of(y * own_rows, 128), own_rows)]
        total[...] = dot(own, value.astype(bf16))
        for index in range(len(pieces)):

            @pl.when(step // share == index)
            def _(index=index):
                total[...] += dot(rest[:, :half_rows], pairs[2 * index][...])
                total[...] += dot(rest[:, half_rows:], pairs[2 * index + 1][...])

        finish(total[...], refs[:count], outs)

    def piece_spec(index):
        return pl.BlockSpec(
            (half_rows, UNIT), lambda g, s: (0, jnp.clip(g - index * share, 0, share - 1))
        )

    return pl.pallas_call(
        kernel,
        grid_spec=pltpu.PrefetchScalarGridSpec(
            num_scalar_prefetch=1,
            grid=(blocks,),
            in_specs=[
                pl.BlockSpec(act.shape, lambda g, s: (0, 0)),
                pl.BlockSpec((own_rows, UNIT), lambda g, s: (0, g)),
            ]
            + [piece_spec(index // 2) for index in range(len(flat))]
            + [pl.BlockSpec((extra.shape[0], UNIT), lambda g, s: (0, g)) for extra in extras]
            + [any_spec()] * len(deps),
            out_specs=[pl.BlockSpec((rows, UNIT), lambda g, s: (0, g))] * len(out_types)
            + [pl.BlockSpec((8, UNIT), lambda g, s: (0, g))],
            scratch_shapes=[pltpu.VMEM((rows, own_rows), bf16), pltpu.VMEM((rows, UNIT), f32)],
        ),
        out_shape=[
            (pltpu.HBM if streamed else jax.ShapeDtypeStruct)((rows, cols), dtype)
            for dtype, streamed in out_types
        ]
        + [jax.ShapeDtypeStruct((8, cols), f32)],
        compiler_params=pltpu.CompilerParams(vmem_limit_bytes=20 << 20),
        name="forward_matmul",
    )(where, act, weight, *flat, *extras, *deps)


def backward_matmul(where, grad, weight, pieces, dtype, deps):
    rows, own_rows = grad.shape[0], weight.shape[0]
    blocks = weight.shape[1] // UNIT
    share = blocks // len(pieces)
    half_rows = pieces[0][0].shape[0]
    flat = [piece for pair in pieces for piece in pair]

    def kernel(where, grad, weight, *refs):
        pairs = refs[: len(flat)]
        out, own, rest = refs[-3:]
        step = pl.program_id(0)
        quarter = own_rows // 4
        y, first = where[0], where[1]

        @pl.when(step == 0)
        def _():
            own[...] = jnp.zeros_like(own)
            rest[...] = jnp.zeros_like(rest)

        own[...] += dot_nt(grad[...], weight[...].astype(bf16))
        for index in range(len(pieces)):

            @pl.when(step // share == index)
            def _(index=index):
                rest[:, :half_rows] += dot_nt(grad[...], pairs[2 * index][...])
                rest[:, half_rows:] += dot_nt(grad[...], pairs[2 * index + 1][...])

        @pl.when(step == blocks - 1)
        def _():
            out[:, pl.ds(pl.multiple_of(y * own_rows, 128), own_rows)] = own[...].astype(dtype)
            for k in range(4):
                at = pl.multiple_of((1 - y) * own_rows + (first ^ k) * quarter, 128)
                part = rest[:, k * quarter : (k + 1) * quarter]
                out[:, pl.ds(at, quarter)] = part.astype(dtype)

    def piece_spec(index):
        return pl.BlockSpec(
            (half_rows, UNIT), lambda g, s: (0, jnp.clip(g - index * share, 0, share - 1))
        )

    return pl.pallas_call(
        kernel,
        grid_spec=pltpu.PrefetchScalarGridSpec(
            num_scalar_prefetch=1,
            grid=(blocks,),
            in_specs=[
                pl.BlockSpec((rows, UNIT), lambda g, s: (0, g)),
                pl.BlockSpec((own_rows, UNIT), lambda g, s: (0, g)),
            ]
            + [piece_spec(index // 2) for index in range(len(flat))]
            + [any_spec()] * len(deps),
            out_specs=pl.BlockSpec((rows, 2 * own_rows), lambda g, s: (0, 0)),
            scratch_shapes=[pltpu.VMEM((rows, own_rows), f32)] * 2,
        ),
        out_shape=jax.ShapeDtypeStruct((rows, 2 * own_rows), dtype),
        compiler_params=pltpu.CompilerParams(vmem_limit_bytes=14 << 20),
        name="backward_matmul",
    )(where, grad, weight, *flat, *deps)


def slope_matmul(where, grad, weight, pieces, slope, deps):
    rows, own_rows = grad.shape[0], weight.shape[0]
    quarter = own_rows // 4

    def kernel(where, grad, weight, half, other, slope, *refs):
        out = refs[-1]
        step = pl.program_id(0)

        @pl.when(step < 4)
        def _():
            out[...] = (dot_nt(grad[...], weight[...].astype(bf16)) * slope[...]).astype(bf16)

        for low, piece in ((4, half), (6, other)):

            @pl.when(jnp.logical_and(step >= low, step < low + 2))
            def _(piece=piece):
                out[...] = (dot_nt(grad[...], piece[...]) * slope[...]).astype(bf16)

    def place(g, s):
        return (0, jnp.where(g < 4, s[0] * 4 + g, (1 - s[0]) * 4 + (s[1] ^ jnp.maximum(g - 4, 0))))

    def piece_spec(low):
        return pl.BlockSpec((quarter, D), lambda g, s: (jnp.clip(g - low, 0, 1), 0))

    return pl.pallas_call(
        kernel,
        grid_spec=pltpu.PrefetchScalarGridSpec(
            num_scalar_prefetch=1,
            grid=(8,),
            in_specs=[
                pl.BlockSpec(grad.shape, lambda g, s: (0, 0)),
                pl.BlockSpec((quarter, D), lambda g, s: (jnp.minimum(g, 3), 0)),
                piece_spec(4),
                piece_spec(6),
                pl.BlockSpec((rows, quarter), place),
            ]
            + [any_spec()] * len(deps),
            out_specs=pl.BlockSpec((rows, quarter), place),
        ),
        out_shape=jax.ShapeDtypeStruct((rows, 2 * own_rows), bf16),
        compiler_params=pltpu.CompilerParams(vmem_limit_bytes=14 << 20),
        name="slope_matmul",
    )(where, grad, weight, *pieces, in_hbm(slope), *deps)


def finish_kernel(where, mine, theirs, *refs):
    grad, sums = refs[-2:]

    @pl.when(pl.program_id(0) == 0)
    def _():
        sums[...] = jnp.zeros_like(sums)

    mine, theirs = mine[...].astype(f32), theirs[...].astype(f32)

    @pl.when(where[0] == 0)
    def _():
        grad[:, :UNIT] = mine
        grad[:, UNIT:] = theirs

    @pl.when(where[0] == 1)
    def _():
        grad[:, :UNIT] = theirs
        grad[:, UNIT:] = mine

    mine, theirs = mine * mine, theirs * theirs
    sums[0:1] += jnp.sum(mine, axis=0, keepdims=True)
    sums[1:2] += jnp.sum(theirs, axis=0, keepdims=True)
    both = mine + theirs
    high = both.astype(bf16)
    low = (both - high.astype(f32)).astype(bf16)
    ones = jnp.ones((8, UNIT), bf16)
    rows = dot_nt(ones, high) + dot_nt(ones, low)
    for step in range(UNIT // BLOCK):

        @pl.when(pl.program_id(0) == step)
        def _(step=step):
            sums[2:3, step * BLOCK : (step + 1) * BLOCK] = rows[:1]


def finish(by_rows, index, mine, theirs, at, shape, grad, core):
    if by_rows:
        place = lambda g, s: (2 * index + g, 0)
    else:
        place = lambda g, s: (g, index)
    piece = pl.BlockSpec((BLOCK, UNIT), lambda g, s: (2 * at + g, 0))
    extra = [] if grad is None else [in_hbm(grad)]
    return pl.pallas_call(
        finish_kernel,
        grid_spec=pltpu.PrefetchScalarGridSpec(
            num_scalar_prefetch=1,
            grid=(UNIT // BLOCK,),
            in_specs=[piece, piece] + [any_spec()] * len(extra),
            out_specs=[
                pl.BlockSpec((BLOCK, 2 * UNIT), place),
                pl.BlockSpec((8, UNIT), lambda g, s: (0, 0)),
            ],
        ),
        out_shape=[pltpu.HBM(shape, f32), jax.ShapeDtypeStruct((8, UNIT), f32)],
        input_output_aliases={3: 0} if extra else {},
        compiler_params=pltpu.CompilerParams(vmem_limit_bytes=10 << 20),
        cost_estimate=pl.CostEstimate(flops=1, bytes_accessed=1, transcendentals=0),
        name="finish",
    )(core.reshape(1), mine, theirs, *extra)


def update_kernel(units, where, *refs):
    pieces = refs[: 2 * units]
    weight, row_factor, col_factor = refs[2 * units : 2 * units + 3]
    weight_new, weight_half = refs[-2:]
    unit = pl.program_id(0) // 2
    for index in range(units):
        for core in range(2):

            @pl.when(jnp.logical_and(unit == index, where[0] == core))
            def _(index=index, core=core):
                sides = pieces[2 * index : 2 * index + 2]
                for side in range(2):
                    at = slice(side * UNIT, (side + 1) * UNIT)
                    grad = sides[side ^ core][...].astype(f32)
                    new = weight[:, at] - grad * (row_factor[...] * col_factor[:, at])
                    weight_new[:, at] = new
                    weight_half[:, at] = new.astype(bf16)


def update(by_rows, pieces, weight, row_factor, col_factor, core):
    units = len(pieces)
    if by_rows:
        place = lambda g, s: (g, 0)
        row_place = lambda g, s: (g, 0)
        col_place = lambda g, s: (0, 0)
    else:
        place = lambda g, s: (g % 2, g // 2)
        row_place = lambda g, s: (g % 2, 0)
        col_place = lambda g, s: (0, g // 2)

    def piece_spec(index, at):
        return pl.BlockSpec(
            (BLOCK, UNIT), lambda g, s: (2 * at + jnp.clip(g - 2 * index, 0, 1), 0)
        )

    specs, values = [], []
    for index, (mine, theirs, at) in enumerate(pieces):
        specs += [piece_spec(index, at)] * 2
        values += [in_hbm(mine), in_hbm(theirs)]
    block = pl.BlockSpec((BLOCK, 2 * UNIT), place)
    shape = weight.shape
    return pl.pallas_call(
        partial(update_kernel, units),
        grid_spec=pltpu.PrefetchScalarGridSpec(
            num_scalar_prefetch=1,
            grid=(2 * units,),
            in_specs=specs
            + [
                block,
                pl.BlockSpec((BLOCK, 1), row_place),
                pl.BlockSpec((1, 2 * UNIT), col_place),
            ],
            out_specs=[block, block],
        ),
        out_shape=[pltpu.HBM(shape, f32), pltpu.HBM(shape, bf16)],
        compiler_params=pltpu.CompilerParams(vmem_limit_bytes=14 << 20),
        name="update",
    )(core.reshape(1), *values, weight, row_factor, col_factor)


def swap_by(first, axis, mine, theirs):
    return jnp.concatenate(
        [jnp.where(first, mine, theirs), jnp.where(first, theirs, mine)], axis=axis
    )


def call(name, kernel, out_shapes, smem, inputs, deps, held=False):
    place = pltpu.VMEM if held else jax.ShapeDtypeStruct
    if held:
        inputs = [in_vmem(value) for value in inputs]
    count = len(smem) + len(inputs)

    def body(*refs):
        kernel(*refs[:count], *refs[count + len(deps) :])

    return pl.pallas_call(
        body,
        in_specs=[pl.BlockSpec(memory_space=pltpu.SMEM)] * len(smem)
        + [pl.BlockSpec(memory_space=pltpu.VMEM)] * len(inputs)
        + [any_spec()] * len(deps),
        out_specs=[pl.BlockSpec(memory_space=pltpu.VMEM)] * len(out_shapes),
        out_shape=[place(shape, dtype) for shape, dtype in out_shapes],
        compiler_params=pltpu.CompilerParams(vmem_limit_bytes=24 << 20),
        cost_estimate=pl.CostEstimate(flops=1, bytes_accessed=1, transcendentals=0),
        name=name,
    )(*smem, *inputs, *deps)


def ordered(name, values, shape, deps):
    def kernel(*refs):
        out = refs[-1]
        at = 0
        for ref in refs[:-1]:
            rows = ref.shape[0]
            out[at : at + rows] = ref[...].astype(bf16)
            at += rows

    return call(name, kernel, [(shape, bf16)], [], values, deps)[0]


class Unit:
    pass


class Torus:
    x_pairs = tuple((i, i ^ 1) for i in range(8))
    z_in = tuple((z * 2 + x, w * 2 + x) for x in range(2) for z, w in ((0, 1), (3, 2)))
    z_mid = tuple((z * 2 + x, w * 2 + x) for x in range(2) for z, w in ((1, 2), (2, 1)))
    z_out = tuple((z * 2 + x, w * 2 + x) for x in range(2) for z, w in ((1, 0), (2, 3)))
    z_swap = z_in + z_out
    planes = [[z * 2, z * 2 + 1, 8 + z * 2, 8 + z * 2 + 1] for z in range(4)]
    sizes = (2, 2, 2, 2, 2, 1, 1)

    def __init__(self, share):
        self.core = lax.axis_index("res")
        place = lax.axis_index("dp")
        self.x = place % 2
        self.z = place // 2
        self.y = lax.axis_index("fsdp")
        self.inner = jnp.logical_or(self.z == 1, self.z == 2)
        self.share = share
        self.share_in = share.reshape(1)
        self.inner_in = self.inner.astype(jnp.int32).reshape(1)
        self.waiting = []
        self.groups = []
        self.later = []
        self.grads = {}
        self.tokens = []
        self.tick = 0
        self.buffers = {}


    def gather_vectors(self, vectors):
        own = vectors.astype(bf16).T
        other = lax.ppermute(own, "fsdp", SWAP)
        return swap_by(self.y == 0, 1, own, other).T

    def gather_all(self, weights):
        first = 2 * self.core + self.x
        self.where = jnp.stack([self.y, first])
        self.weights = [in_hbm(weight) for weight in weights]
        parts = []
        for weight, count in zip(weights, (1, 1, 2, 1)):
            rows, cols = weight.shape[0] // 4, weight.shape[1] // count
            for sub in range(count):
                parts.append(lax.dynamic_slice(weight, (first * rows, sub * cols), (rows, cols)))
        self.from_y = []
        before = []
        for index, part in enumerate(parts):
            if index == 4:
                before = before + [self.from_y[0]]
            part = ordered("cast", [part], part.shape, before)
            before = [part]
            self.from_y.append(lax.ppermute(part, "fsdp", SWAP))
        self.from_x = {0: lax.ppermute(self.from_y[0], "dp", self.x_pairs)}
        self.pieces = {}
        self.squares = {}
        self.to_core(0, before)
        self.to_x(1, [self.from_x[0]])
        self.to_x(2, [self.from_x[0]])
        self.to_x(3, [self.pieces[0][1]])

    def to_x(self, part, after):
        piece = ordered("x_part", [self.from_y[part]], self.from_y[part].shape, after)
        self.from_x[part] = lax.ppermute(piece, "dp", self.x_pairs)

    def to_core(self, part, after):
        piece, from_x = self.from_y[part], self.from_x[part]
        rows, cols = piece.shape
        half = ordered("core_part", [piece, from_x], (2 * rows, cols), after)
        self.pieces[part] = (half, lax.ppermute(half, "res", SWAP))

    def project(self, normed, bias):
        def finish(total, extra, outs):
            outs[0][...] = (total + extra[0][...]).astype(bf16)

        projected, self.squares[0] = forward_matmul(
            finish, self.where, normed, self.weights[0], [self.pieces[0]], [bias[None]], [(bf16, False)], []
        )
        self.to_core(1, [projected])
        return projected

    def attend_out(self, mixed, tokens, bias):
        self.to_core(2, [mixed])
        self.to_core(3, [mixed, self.pieces[2][0]])
        self.to_x(4, [mixed])

        def finish(total, extra, outs):
            outs[0][...] = extra[0][...] + (total + extra[1][...])

        middle, self.squares[1] = forward_matmul(
            finish,
            self.where,
            mixed,
            self.weights[1],
            [self.pieces[1]],
            [tokens, bias[None]],
            [(f32, False)],
            [],
        )
        return middle

    def feed_up(self, normed, bias):
        def finish(total, extra, outs):
            outs[0][...], outs[1][...] = gelu_parts(total + extra[0][...])

        pieces = [self.pieces[2], self.pieces[3]]
        hidden, slope, self.squares[2] = forward_matmul(
            finish, self.where, normed, self.weights[2], pieces, [bias[None]], [(bf16, False), (f32, True)], []
        )
        self.to_core(4, [hidden])
        return hidden, slope

    def feed_down(self, hidden, middle, bias):
        def finish(total, extra, outs):
            outs[0][...] = (extra[0][...] + (total + extra[1][...])).astype(bf16)

        output, self.squares[3] = forward_matmul(
            finish,
            self.where,
            hidden,
            self.weights[3],
            [self.pieces[4]],
            [middle, bias[None]],
            [(bf16, False)],
            [self.tokens[0]],
        )
        self.require(in_hbm(output), 2)
        return output

    def back_down(self, grad, slope):
        return slope_matmul(
            self.where, grad, self.weights[3], self.pieces[4], slope, [self.tokens[0]]
        )

    def back_up(self, grad):
        pieces = [self.pieces[2], self.pieces[3]]
        return backward_matmul(self.where, grad, self.weights[2], pieces, f32, [self.tokens[1]])

    def back_out(self, grad):
        return backward_matmul(
            self.where, grad, self.weights[1], [self.pieces[1]], bf16, [self.fence(2)]
        )

    def back_project(self, grad):
        return backward_matmul(
            self.where, grad, self.weights[0], [self.pieces[0]], f32, [self.fence(5)]
        )


    def after(self, value, tick):
        return value + self.tokens[tick][0, 0]

    def fence(self, tick):
        return lax.ppermute(self.tokens[tick], "res", SWAP)

    def held_out(self, value):
        return in_hbm(value)

    def require(self, value, tick):
        self.later.append((tick, value))

    def push(self, by_rows, left, right):
        half = left.shape[1] // 2
        low, high = left[:, :half], left[:, half:]
        own = jnp.where(self.y == 0, low, high)
        other = jnp.where(self.y == 0, high, low)
        count = half // UNIT if by_rows else right.shape[1] // (2 * UNIT)
        units = []
        for index in range(count):
            unit = Unit()
            unit.by_rows, unit.index, unit.matrix = by_rows, index, units
            unit.shape = (half, right.shape[1])
            if by_rows:
                at = index * UNIT
                unit.own, unit.other = own[:, at : at + UNIT], other[:, at : at + UNIT]
                cols = right
            else:
                unit.own, unit.other = own, other
                cols = right[:, index * 2 * UNIT : (index + 1) * 2 * UNIT]
            unit.kept = jnp.where(self.core == 0, cols[:, :UNIT], cols[:, UNIT:])
            unit.sent = jnp.where(self.core == 0, cols[:, UNIT:], cols[:, :UNIT])
            units.append(unit)
        for unit in units:
            self.waiting.append(unit)
            if len(self.waiting) == self.sizes[len(self.groups)]:
                self.groups.append(self.waiting)
                self.waiting = []
                self.begin(len(self.groups) - 1, self.tokens[-1:])
                if len(self.groups) > 1:
                    self.step()
        return units

    def group(self, index):
        return self.groups[index] if 0 <= index < len(self.groups) else []

    def begin(self, index, deps):
        units = self.group(index)
        values = []
        for unit in units:
            values += [unit.own, unit.other, unit.kept, unit.sent]

        def kernel(share, *refs):
            sent_out, own_out, other_out = refs[-3:]
            for k in range(len(units)):
                own, other, kept, sent = (ref[...] for ref in refs[4 * k : 4 * k + 4])
                rows = slice(k * UNIT, (k + 1) * UNIT)
                own_out[rows] = (share[0] * dot_tn(own, kept)).astype(bf16)
                other_out[rows] = (share[0] * dot_tn(other, kept)).astype(bf16)
                at = 2 * k * UNIT
                sent_out[at : at + UNIT] = (share[0] * dot_tn(own, sent)).astype(bf16)
                at += UNIT
                sent_out[at : at + UNIT] = (share[0] * dot_tn(other, sent)).astype(bf16)

        rows = len(units) * UNIT
        shapes = [((2 * rows, UNIT), bf16), ((rows, UNIT), bf16), ((rows, UNIT), bf16)]
        sent, own, other = call("k_m", kernel, shapes, [self.share_in], values, deps, True)
        self.buffers["own", index] = own
        self.buffers["other", index] = other
        self.buffers["from_core", index] = lax.ppermute(sent, "res", SWAP)

    def step(self):
        tick = self.tick
        buffers = self.buffers
        sizes = [len(self.group(tick - k)) for k in range(6)]
        size_y, size_x, size_a, size_b, size_c, size_d = sizes
        both = max(size_a, size_c)
        names, values, out_rows = [], [], []

        def give(name, key, index):
            names.append(name)
            values.append(buffers[key, index])

        if size_y:
            give("y_kept", "other", tick)
            give("y_core", "from_core", tick)
            out_rows.append(("for_y", size_y))
        if size_x:
            give("x_kept", "own", tick - 1)
            give("x_core", "from_core", tick - 1)
            give("x_y", "from_y", tick - 1)
            out_rows.append(("for_x", size_x))
        if size_a:
            give("a_kept", "for_x", tick - 1)
            give("a_new", "from_x", tick - 1)
            out_rows.append(("v1", size_a))
        if size_b:
            give("b_kept", "v1", tick - 1)
            give("swapped", "from_swap", tick - 1)
            out_rows.append(("v2", size_b))
        if size_c:
            give("c_kept", "v2", tick - 1)
            give("c_new", "from_mid", tick - 1)
            out_rows.append(("v3", size_c))
        if both:
            out_rows.append(("swap", both))
        if size_d:
            give("d_kept", "v3", tick - 1)
            if not size_b:
                give("swapped", "from_swap", tick - 1)
            out_rows.append(("final", size_d))
        out_names = [name for name, _ in out_rows] + ["token"]

        def kernel(inner, *refs):
            ins = dict(zip(names, refs))
            outs = dict(zip(out_names, refs[len(names) :]))
            outs["token"][...] = jnp.zeros_like(outs["token"])
            for k in range(size_y):
                rows = slice(k * UNIT, (k + 1) * UNIT)
                at = (2 * k + 1) * UNIT
                outs["for_y"][rows] = ins["y_kept"][rows] + ins["y_core"][at : at + UNIT]
            for k in range(size_x):
                rows = slice(k * UNIT, (k + 1) * UNIT)
                at = 2 * k * UNIT
                total = ins["x_kept"][rows].astype(f32) + ins["x_core"][at : at + UNIT].astype(f32)
                outs["for_x"][rows] = (total + ins["x_y"][rows].astype(f32)).astype(bf16)

            def add(kept, new, out, size):
                rows = slice(0, size * UNIT)
                outs[out][...] = ins[kept][rows] + ins[new][rows]

            if size_a:
                add("a_kept", "a_new", "v1", size_a)

                @pl.when(inner[0] == 0)
                def _():
                    outs["swap"][: size_a * UNIT] = outs["v1"][...]

            if size_b:
                add("b_kept", "swapped", "v2", size_b)
            if size_c:
                add("c_kept", "c_new", "v3", size_c)

                @pl.when(inner[0] == 1)
                def _():
                    outs["swap"][: size_c * UNIT] = outs["v3"][...]

            if size_d:

                @pl.when(inner[0] == 1)
                def _():
                    outs["final"][...] = ins["d_kept"][...]

                @pl.when(inner[0] == 0)
                def _():
                    outs["final"][...] = ins["swapped"][: size_d * UNIT]

        shapes = [((rows * UNIT, UNIT), bf16) for _, rows in out_rows] + [((8, 128), f32)]
        deps = self.tokens[-1:]
        deps += [value for when, value in self.later if when == tick]
        outs = dict(zip(out_names, call("t", kernel, shapes, [self.inner_in], values, deps, True)))
        self.tokens.append(outs["token"])
        for name in ("for_x", "v1", "v2", "v3"):
            if name in outs:
                buffers[name, tick] = outs[name]
        if size_y:
            buffers["from_y", tick] = lax.ppermute(outs["for_y"], "fsdp", SWAP)
        if size_x:
            buffers["from_x", tick] = lax.ppermute(outs["for_x"], "dp", self.x_pairs)
        if both:
            buffers["from_swap", tick] = lax.ppermute(outs["swap"], "dp", self.z_swap)
        if size_b:
            buffers["from_mid", tick] = lax.ppermute(outs["v2"], "dp", self.z_mid)
        if size_d:
            final = outs["final"]
            received = lax.ppermute(final, "res", SWAP)
            ended = self.group(tick - 5)
            for k, unit in enumerate(ended):
                unit.piece = (final, received, k)
                grad = self.grads.get(id(unit.matrix))
                grad, sums = finish(
                    unit.by_rows, unit.index, final, received, k, unit.shape, grad, self.core
                )
                self.grads[id(unit.matrix)] = grad
                unit.cols, unit.rows = (sums[0], sums[1]), sums[2]
                self.later.append((tick + 2, sums))
        self.tick += 1

    def update(self, by_rows, units, weight, rows, cols, index):
        pieces = [unit.piece for unit in units]
        row_sums = [unit.rows for unit in units]
        col_sums = [swap_by(self.core == 0, 0, *unit.cols) for unit in units]
        square_total = jnp.sum(self.squares[index])
        full_rows = 2 * weight.shape[0]
        row_sum = jnp.concatenate(row_sums) if by_rows else sum(row_sums)
        col_sum = sum(col_sums) if by_rows else jnp.concatenate(col_sums)
        rows_new = DECAY * rows + (1.0 - DECAY) * (row_sum / weight.shape[1] + EPS_SQUARE)
        both = jnp.concatenate([col_sum, jnp.stack([jnp.sum(rows_new), square_total])])
        both = both + lax.ppermute(both, "fsdp", SWAP)
        cols_new = DECAY * cols + (1.0 - DECAY) * (both[:-2] / full_rows + EPS_SQUARE)
        row_mean = both[-2] / full_rows
        scale = jnp.sqrt(both[-1] / (full_rows * weight.shape[1]) + EPS_WEIGHT)
        row_factor = RATE * scale * lax.rsqrt(rows_new / row_mean)
        col_factor = lax.rsqrt(cols_new)
        new, half = update(
            by_rows, pieces, in_hbm(weight), row_factor[:, None], col_factor[None, :], self.core
        )
        grad = self.grads[id(units)]
        return [grad, rows_new, cols_new, new, half]

    def vectors_step(self):
        step, value = self.vectors
        deps = self.tokens[-1:]

        def total(kernel, values, shape):
            return call("vectors", kernel, [(shape, f32)], [], values, deps)[0]

        def add(mine, theirs, out):
            out[...] = mine[...] + theirs[...]

        if step > 0:
            kept, received = value
            if step == 6:
                return jnp.where(self.inner, kept, received)
            value = total(add, [kept, received], kept.shape)
        else:
            value = total(lambda mine, out: out.__setitem__(..., mine[...]), [value], value.shape)
        kept = sent = value
        if step == 1:
            half = value.shape[1] // 2
            low, high = value[:, :half], value[:, half:]
            kept = jnp.where(self.y == 0, low, high)
            sent = jnp.where(self.y == 0, high, low)
        axis = ("res", "fsdp", "dp", "dp", "dp", "dp")[step]
        pairs = (SWAP, SWAP, self.x_pairs, self.z_in, self.z_mid, self.z_out)[step]
        received = lax.ppermute(sent, axis, pairs)
        self.require(received, self.tick)
        self.vectors = (step + 1, (kept, received))

    def begin_vectors(self, grad):
        self.vectors = (0, grad)

    def pair_sum(self, value):
        return value + lax.ppermute(value, "fsdp", SWAP)


class AnyMesh:
    def __init__(self, share):
        self.share = share

    def after(self, value, tick):
        return value

    def gather_vectors(self, vectors):
        return lax.all_gather(vectors.astype(bf16), "fsdp", axis=0, tiled=True)

    def gather_all(self, weights):
        self.weights = [self.gather_vectors(weight) for weight in weights]

    def project(self, normed, bias):
        return (dot(normed, self.weights[0]) + bias).astype(bf16)

    def attend_out(self, mixed, tokens, bias):
        return tokens + (dot(mixed, self.weights[1]) + bias)

    def feed_up(self, normed, bias):
        return gelu_parts(dot(normed, self.weights[2]) + bias)

    def feed_down(self, hidden, middle, bias):
        return (middle + (dot(hidden, self.weights[3]) + bias)).astype(bf16)

    def back_down(self, grad, slope):
        return (dot_nt(grad, self.weights[3]) * slope).astype(bf16)

    def back_up(self, grad):
        return dot_nt(grad, self.weights[2])

    def back_out(self, grad):
        return dot_nt(grad, self.weights[1]).astype(bf16)

    def back_project(self, grad):
        return dot_nt(grad, self.weights[0])

    def push(self, by_rows, left, right):
        grad = self.share * dot_tn(left, right)
        grad = lax.psum_scatter(grad, "fsdp", scatter_dimension=0, tiled=True)
        return lax.psum(grad, ("res", "dp"))

    def held_out(self, value):
        return value

    def require(self, value, tick):
        pass

    def step(self):
        pass

    def begin_vectors(self, grad):
        grad = lax.psum_scatter(grad, "fsdp", scatter_dimension=1, tiled=True)
        self.vectors = lax.psum(grad, ("res", "dp"))

    def vectors_step(self):
        return self.vectors

    def pair_sum(self, value):
        return lax.psum(value, "fsdp")

    def update(self, by_rows, grad, weight, rows, cols, index):
        square_total = jnp.sum(weight * weight)
        full_rows = weight.shape[0] * lax.axis_size("fsdp")
        square = grad * grad + EPS_SQUARE
        rows_new = DECAY * rows + (1.0 - DECAY) * jnp.mean(square, axis=1)
        col_sum, row_total, weight_total = self.pair_sum(
            (jnp.sum(square, axis=0), jnp.sum(rows_new), square_total)
        )
        cols_new = DECAY * cols + (1.0 - DECAY) * col_sum / full_rows
        row_mean = row_total / full_rows
        scale = jnp.sqrt(weight_total / (full_rows * weight.shape[1]) + EPS_WEIGHT)
        estimate = rows_new[:, None] * cols_new[None, :] / row_mean
        weight_new = weight - RATE * scale * grad * lax.rsqrt(estimate)
        return [grad, rows_new, cols_new, weight_new, weight_new.astype(bf16)]


def on_device(
    special,
    tokens_in,
    cotangent,
    crop_counts,
    group_tokens,
    weight_qkv,
    rows_qkv,
    cols_qkv,
    weight_out,
    rows_out,
    cols_out,
    weight_up,
    rows_up,
    cols_up,
    weight_down,
    rows_down,
    cols_down,
    vectors,
    moment_vec,
):
    group = lax.axis_index("res")
    rows = tokens_in.shape[0]
    total = (group_tokens[0] + group_tokens[1]).astype(f32)
    share = jnp.where(group == 0, group_tokens[0], group_tokens[1]).astype(f32) / total
    comm = (Torus if special else AnyMesh)(share)
    segment = segment_ids(crop_counts.reshape(2), group, rows)
    valid = (segment < padding_label).astype(f32)
    tokens = tokens_in.astype(f32)
    grad_output = cotangent.astype(f32) * valid[:, None]
    grad_second = grad_output.astype(bf16)

    vector_half = comm.gather_vectors(vectors)
    comm.gather_all((weight_qkv, weight_out, weight_up, weight_down))
    (
        query_bias,
        value_bias,
        out_bias,
        up_bias,
        down_bias,
        gain_one,
        shift_one,
        gain_two,
        shift_two,
    ) = unpack(vector_half.astype(f32))

    normed, norm_back_one = jax.vjp(norm_forward, tokens, gain_one, shift_one)
    normed = normed.astype(bf16)
    bias_qkv = jnp.concatenate([query_bias, jnp.zeros_like(query_bias), value_bias])
    projected = comm.project(normed, bias_qkv)
    mixed = attend(segment, projected)
    middle = comm.attend_out(mixed, tokens, out_bias)
    normed_two, norm_back_two = jax.vjp(norm_forward, middle, gain_two, shift_two)
    normed_two = normed_two.astype(bf16)
    hidden, slope = comm.feed_up(normed_two, up_bias)
    down_grad = comm.push(True, hidden, grad_second)
    output = comm.feed_down(hidden, middle, down_bias)

    grad_before = comm.back_down(grad_second, slope)
    up_grad = comm.push(False, normed_two, grad_before)
    grad_normed_two = comm.back_up(grad_before)
    grad_middle_part, grad_gain_two, grad_shift_two = norm_back_two(grad_normed_two)
    grad_middle = grad_output + grad_middle_part
    grad_branch = grad_middle.astype(bf16)
    grad_mixed = comm.back_out(grad_branch)
    grad_projected = attend_back(segment, projected, grad_mixed)
    qkv_grad = comm.push(False, normed, grad_projected)
    out_grad = comm.push(False, mixed, grad_branch)
    grad_normed = lax.optimization_barrier(comm.back_project(grad_projected))
    grad_tokens_part, grad_gain_one, grad_shift_one = norm_back_one(grad_normed)
    grad_tokens = grad_middle + grad_tokens_part

    def column_sum(value):
        return jnp.sum(value.astype(f32), axis=0)

    bias_qkv_grad = column_sum(grad_projected)
    vec_grad = share * jnp.concatenate(
        [
            bias_qkv_grad[None, :D],
            bias_qkv_grad[None, 2 * D :],
            column_sum(grad_branch)[None],
            column_sum(grad_before).reshape(FF // D, D),
            column_sum(grad_second)[None],
            grad_gain_one[None],
            grad_shift_one[None],
            grad_gain_two[None],
            grad_shift_two[None],
        ],
        axis=0,
    )
    comm.require(grad_tokens, 7)
    comm.begin_vectors(vec_grad)
    comm.step()
    comm.vectors_step()
    down = comm.update(True, down_grad, weight_down, rows_down, cols_down, 3)
    comm.require(comm.held_out(down[-1]), 8)
    comm.step()
    comm.vectors_step()
    comm.step()
    comm.vectors_step()
    up = comm.update(False, up_grad, weight_up, rows_up, cols_up, 2)
    comm.require(comm.held_out(up[-1]), 10)
    comm.step()
    comm.vectors_step()
    comm.step()
    comm.vectors_step()
    qkv = comm.update(False, qkv_grad, weight_qkv, rows_qkv, cols_qkv, 0)
    comm.require(comm.held_out(qkv[-1]), 11)
    comm.step()
    comm.vectors_step()
    grad_vec = comm.vectors_step().T
    moment_new = DECAY * moment_vec + (1.0 - DECAY) * (grad_vec * grad_vec + EPS_SQUARE)
    square_sum = comm.pair_sum(jnp.sum(vectors * vectors, axis=0))
    vector_scale = jnp.sqrt(square_sum / D + EPS_WEIGHT)
    vectors_new = vectors - RATE * vector_scale[None, :] * grad_vec * lax.rsqrt(moment_new)
    out = comm.update(False, out_grad, weight_out, rows_out, cols_out, 1)
    return tuple(
        [output, grad_tokens]
        + qkv
        + out
        + up
        + down
        + [grad_vec, moment_new, vectors_new, vectors_new.astype(bf16)]
    )


def solution(mesh):
    special = mesh.shape["fsdp"] == 2 and mesh.shape["dp"] == 8
    token_rows = P(("res", "dp", "fsdp"), None)
    matrix_in = (P("fsdp", None), P("fsdp"), P())
    matrix_out = (P("fsdp", None), P("fsdp"), P(), P("fsdp", None), P("fsdp", None))
    return jax.shard_map(
        partial(on_device, special),
        mesh=mesh,
        in_specs=(token_rows, token_rows, P("res", "dp", "fsdp", None), P())
        + matrix_in * 4
        + (P("fsdp", None), P("fsdp", None)),
        out_specs=(token_rows, token_rows) + matrix_out * 4 + (P("fsdp", None),) * 4,
        check_vma=False,
    )
```

time: 1510 us -> 470 us (0.31)
  waiting for transfers between devices: 1190 us -> 116 us
  Pallas kernels: 0 us -> 186 us
  matrix products: 89.8 us -> 0 us
  blocking collectives: 78.1 us -> 0 us
  starting transfers between devices: 0.63 us -> 76.6 us
  other arithmetic: 90.5 us -> 29.7 us
  local copies, waits for them, and re-layouts: 25.9 us -> 43.2 us
    reduce_scatter x5 -> x0, waiting for transfers between devices: 536 us -> none  [the longest x1 192 us: on_device(): lax.psum_scatter(weighted[2], 'fsdp', scatter_dimension=0, tiled=True)]
    psum x1 -> x0, waiting for transfers between devices: 385 us -> none  [on_device(): lax.psum((shards[0], shards[1], shards[2], shards[3], shards[4]), ('res',...]
    all_gather x4 -> x0, waiting for transfers between devices: 265 us -> none  [the longest x1 103 us: on_device(): lax.all_gather(weight_up.astype(jnp.bfloat16), 'fsdp', axis=0, tiled=True)]
    pallas_call x0 -> x65, Pallas kernels: none -> 186 us  [the longest x41 64.4 us: call(): pl.pallas_call(body, in_specs=[pl.BlockSpec(memory_space=pltpu.SMEM)] * l...]
    ppermute x0 -> x73, waiting for transfers between devices: none -> 116 us  [the longest x7 65.3 us: step(): buffers['from_y', tick] = lax.ppermute(outs['for_y'], 'fsdp', SWAP)]
    dot_general x18 -> x0, matrix products: 89.8 us -> none  [the longest x1 16.5 us: forward(): jnp.dot(normed_two, weight_up, preferred_element_type=jnp.float32) + up_bias]
    ppermute x0 -> x73, starting transfers between devices: none -> 76.6 us  [the longest x9 23 us: step(): buffers['from_swap', tick] = lax.ppermute(outs['swap'], 'dp', self.z_swap)]
    psum x2 -> x0, blocking collectives: 72.7 us -> none  [the longest x1 64.3 us: on_device(): lax.psum((shards[0], shards[1], shards[2], shards[3], shards[4]), ('res',...]
  transfers between devices with their start and end apart: 10 -> 73, of which waited for: 10 -> 29; matrix products, arithmetic and copies ran while one was open for 8% -> 9% of each run, Pallas kernels for 0% -> 39%
where the time goes in v1:
time: 470 us; the launch traced here: 463 us
  Pallas kernels  186 us (40%)
  waiting for transfers between devices  116 us (25%)
  starting transfers between devices  76.6 us (16%)
  local copies, waits for them, and re-layouts  43.2 us (9%)
  other arithmetic  29.7 us (6%)
  between operations  12.3 us (3%)
    ppermute x7, waiting for transfers between devices, step(): buffers['from_y', tick] = lax.ppermute(outs['for_y'], 'fsdp', SWAP)  65.3 us
    pallas_call x41, Pallas kernels, call(): pl.pallas_call(body, in_specs=[pl.BlockSpec(memory_space=pltpu.SMEM)] * l...  64.4 us
    pallas_call x4, Pallas kernels, update(): pl.pallas_call(partial(update_kernel, units), grid_spec=pltpu.PrefetchSca...  34.7 us
    pallas_call x4, Pallas kernels, forward_matmul(): pl.pallas_call(kernel, grid_spec=pltpu.PrefetchScalarGridSpec(num_scalar_...  29.3 us
    unnamed x284, local copies, waits for them, and re-layouts  26.3 us
    pallas_call x12, Pallas kernels, finish(): pl.pallas_call(finish_kernel, grid_spec=pltpu.PrefetchScalarGridSpec(num_...  26.1 us
    ppermute x9, starting transfers between devices, step(): buffers['from_swap', tick] = lax.ppermute(outs['swap'], 'dp', self.z_swap)  23 us
    pallas_call x3, Pallas kernels, backward_matmul(): pl.pallas_call(kernel, grid_spec=pltpu.PrefetchScalarGridSpec(num_scalar_...  21.4 us
  transfers between devices with their start and end apart: 73, of which 29 were waited for; matrix products, arithmetic and copies ran while one was open for 9% of the time, Pallas kernels for 39%

profile of v1, /device:TPU:0, one launch (start us, length us, event | category | flops | bytes accessed | tf_op | source)
XLA Modules:
  0.0 463.5 jit_solution(7616004445407839141)
XLA Ops:
  2.4 3.0 collective-permute-start.1
  10.5 13.2 %collective-permute-done.1.refs_2_.refs_0_ = bf16[128,3072]{1,0:T(8,128)(2,1)S(1)} collective-permute-done((bf16[128,3072]{1,0:T(8,128)(2,1)S(1)}, bf16[128,3072]{1,0:T(8,128)(2,1)S(1)}, u32[]{:S(2)}, u32[]{:S(2)}) %collective-permute-start.1) | collective-permute-done | bytes 786464 | tf_op jit(solution)/shard_map/ppermute | solution.py:553
  37.9 3.7 collective-permute-done.2.refs_1_
  61.8 7.3 %forward_matmul.4 = (bf16[256,3072]{1,0:T(8,128)(2,1)S(1)}, f32[8,3072]{1,0:T(8,128)S(1)}) custom-call(s32[2]{0:T(128)S(1)} %pad_add_fusion.where, bf16[256,1024]{1,0:T(8,128)(2,1)S(1)} %add_convert_fusion.1.act, f32[512,3072]{1,0:T(8,128)} %refs_6_.1, bf16[256,3072]{1,0:T(8,128)(2,1)S(1)} %core_part.5.refs_0_, bf16[256,3072]{1,0:T(8,128)(2,1)S(1)} %copy-done.19, ...), custom_call_target="tpu_custom_call" | custom-call | tf_op jit(solution)/shard_map/forward_matmul/pallas_call | solution.py:209
  79.7 3.5 collective-permute-done.11.refs_1_
  89.7 3.3 forward_matmul.5
  96.3 11.9 %forward_matmul.6 = (bf16[256,4096]{1,0:T(8,128)(2,1)S(1)}, f32[256,4096]{1,0:T(8,128)}, f32[8,4096]{1,0:T(8,128)S(1)}) custom-call(s32[2]{0:T(128)S(1)} %copy-done.85, bf16[256,1024]{1,0:T(8,128)(2,1)S(1)} %add_convert_fusion.act, f32[512,4096]{1,0:T(8,128)} %refs_8_.3, bf16[256,2048]{1,0:T(8,128)(2,1)S(1)} %core_part.7.refs_3_.refs_0_, ...), custom_call_target="tpu_custom_call" | custom-call | tf_op jit(solution)/shard_map/forward_matmul/pallas_call | solution.py:209
  125.2 10.0 %slope_matmul.1.grad = bf16[256,4096]{1,0:T(8,128)(2,1)S(1)} custom-call(s32[2]{0:T(128)S(1)} %copy-done.86, bf16[256,1024]{1,0:T(8,128)(2,1)S(1)} %copy-done.27, f32[2048,1024]{1,0:T(8,128)} %refs_8_.2, bf16[1024,1024]{1,0:T(8,128)(2,1)S(1)} %core_part.9.refs_0_.half, bf16[1024,1024]{1,0:T(8,128)(2,1)} %collective-permute-done.15.refs_1_.other, ...), custom_call_target="tpu_custom_call" | custom-call | tf_op jit(solution)/shard_map/slope_matmul/pallas_call | solution.py:319
  136.7 12.9 %collective-permute-done.18.refs_5_ = bf16[1024,512]{1,0:T(8,128)(2,1)S(1)} collective-permute-done((bf16[1024,512]{1,0:T(8,128)(2,1)S(1)}, bf16[1024,512]{1,0:T(8,128)(2,1)S(1)}, u32[]{:S(2)}, u32[]{:S(2)}) %collective-permute-start.18) | collective-permute-done | bytes 1048608 | tf_op jit(solution)/shard_map/ppermute | solution.py:816
  154.6 6.8 %forward_matmul.7 = (bf16[256,1024]{1,0:T(8,128)(2,1)}, f32[8,1024]{1,0:T(8,128)S(1)}) custom-call(s32[2]{0:T(128)S(1)} %copy-done.86, bf16[256,4096]{1,0:T(8,128)(2,1)S(1)} %copy-done.1, f32[2048,1024]{1,0:T(8,128)} %refs_8_.2, bf16[1024,1024]{1,0:T(8,128)(2,1)S(1)} %core_part.9.refs_0_.half, bf16[1024,1024]{1,0:T(8,128)(2,1)} %collective-permute-done.15.refs_1_.other, ...), custom_call_target="tpu_custom_call" | custom-call | tf_op jit(solution)/shard_map/forward_matmul/pallas_call | solution.py:209
  162.9 9.8 %backward_matmul.3 = f32[256,1024]{1,0:T(8,128)S(1)} custom-call(s32[2]{0:T(128)S(1)} %copy-done.86, bf16[256,4096]{1,0:T(8,128)(2,1)S(1)} %slope_matmul.1.grad, f32[512,4096]{1,0:T(8,128)} %refs_8_.3, bf16[256,2048]{1,0:T(8,128)(2,1)S(1)} %copy-done.13, bf16[256,2048]{1,0:T(8,128)(2,1)} %collective-permute-done.9.refs_1_, bf16[256,2048]{1,0:T(8,128)(2,1)S(1)} %copy-done.22, ...), custom_call_target="tpu_custom_call" | custom-call | tf_op jit(solution)/shard_map/backward_matmul/pallas_call | solution.py:275
  184.4 3.8 backward_matmul.4.refs_3_
  188.3 9.0 %attend_back.1.grad = bf16[256,3072]{1,0:T(8,128)(2,1)S(1)} custom-call(s32[256,1]{1,0:T(8,128)S(1)} %fusion.2.refs_0_, s32[1,256]{1,0:T(1,128)S(1)} %copy-done.94, bf16[256,3072]{1,0:T(8,128)(2,1)S(1)} %copy-done.15, bf16[256,1024]{1,0:T(8,128)(2,1)S(1)} %backward_matmul.4.refs_3_), custom_call_target="tpu_custom_call" | custom-call | flops 1 | bytes 1 | tf_op jit(solution)/shard_map/attend_back/pallas_call | solution.py:475
  198.7 6.7 %collective-permute-done.24.refs_5_ = bf16[1024,512]{1,0:T(8,128)(2,1)S(1)} collective-permute-done((bf16[1024,512]{1,0:T(8,128)(2,1)S(1)}, bf16[1024,512]{1,0:T(8,128)(2,1)S(1)}, u32[]{:S(2)}, u32[]{:S(2)}) %collective-permute-start.24) | collective-permute-done | bytes 1048608 | tf_op jit(solution)/shard_map/ppermute | solution.py:816
  213.7 19.2 %collective-permute-done.29.refs_5_ = bf16[1024,512]{1,0:T(8,128)(2,1)S(1)} collective-permute-done((bf16[1024,512]{1,0:T(8,128)(2,1)S(1)}, bf16[1024,512]{1,0:T(8,128)(2,1)S(1)}, u32[]{:S(2)}, u32[]{:S(2)}) %collective-permute-start.29) | collective-permute-done | bytes 1048608 | tf_op jit(solution)/shard_map/ppermute | solution.py:816
  237.3 4.6 collective-permute-start.35
  244.5 15.0 %collective-permute-done.33.refs_5_ = bf16[1024,512]{1,0:T(8,128)(2,1)S(1)} collective-permute-done((bf16[1024,512]{1,0:T(8,128)(2,1)S(1)}, bf16[1024,512]{1,0:T(8,128)(2,1)S(1)}, u32[]{:S(2)}, u32[]{:S(2)}) %collective-permute-start.33) | collective-permute-done | bytes 1048608 | tf_op jit(solution)/shard_map/ppermute | solution.py:816
  268.3 3.6 collective-permute-start.41
  278.3 7.8 %backward_matmul.5 = f32[256,1024]{1,0:T(8,128)S(1)} custom-call(s32[2]{0:T(128)S(1)} %copy-done.86, bf16[256,3072]{1,0:T(8,128)(2,1)S(1)} %attend_back.1.grad, f32[512,3072]{1,0:T(8,128)} %refs_6_.1, bf16[256,3072]{1,0:T(8,128)(2,1)S(1)} %copy-done.17, bf16[256,3072]{1,0:T(8,128)(2,1)S(1)} %copy-done.20, f32[8,128]{1,0:T(8,128)S(1)} %collective-permute-done.37.refs_2_), custom_call_target="tpu_custom_call" | custom-call | tf_op jit(solution)/shard_map/backward_matmul/pallas_call | solution.py:275
  286.6 3.5 collective-permute-done.39.refs_5_
  291.6 5.2 %t.18 = (bf16[512,512]{1,0:T(8,128)(2,1)S(1)}, bf16[512,512]{1,0:T(8,128)(2,1)S(1)}, bf16[1024,512]{1,0:T(8,128)(2,1)S(1)}, bf16[1024,512]{1,0:T(8,128)(2,1)}, b...) custom-call(s32[1]{0:T(128)} %bitcast.16.refs_0_, ...), custom_call_target="tpu_custom_call" | custom-call | flops 1 | bytes 1 | tf_op jit(solution)/shard_map/t/pallas_call | solution.py:475
  298.5 3.6 collective-permute-start.45
  314.0 5.2 %collective-permute-done.43.refs_3_ = bf16[512,512]{1,0:T(8,128)(2,1)S(1)} collective-permute-done((bf16[512,512]{1,0:T(8,128)(2,1)}, bf16[512,512]{1,0:T(8,128)(2,1)S(1)}, u32[]{:S(2)}, u32[]{:S(2)}) %collective-permute-start.43) | collective-permute-done | bytes 524320 | tf_op jit(solution)/shard_map/ppermute | solution.py:816
  322.0 4.2 t.19
  327.6 3.7 collective-permute-start.50
  347.5 11.3 %update.4 = (f32[2048,1024]{1,0:T(8,128)}, bf16[2048,1024]{1,0:T(8,128)(2,1)}) custom-call(s32[1]{0:T(128)} %bitcast.20.where, bf16[1024,512]{1,0:T(8,128)(2,1)} %copy-done.6, bf16[1024,512]{1,0:T(8,128)(2,1)} %copy-done.8, bf16[1024,512]{1,0:T(8,128)(2,1)} %copy-done.6, bf16[1024,512]{1,0:T(8,128)(2,1)} %copy-done.8, ...), custom_call_target="tpu_custom_call" | custom-call | tf_op jit(solution)/shard_map/update/pallas_call | solution.py:441
  358.9 3.5 t.20
  382.7 8.3 %collective-permute-done.55.refs_2_ = bf16[1024,512]{1,0:T(8,128)(2,1)} collective-permute-done((bf16[1024,512]{1,0:T(8,128)(2,1)}, bf16[1024,512]{1,0:T(8,128)(2,1)}, u32[]{:S(2)}, u32[]{:S(2)}) %collective-permute-start.55) | collective-permute-done | bytes 1048608 | tf_op jit(solution)/shard_map/ppermute | solution.py:820
  405.3 11.4 %update.5 = (f32[512,4096]{1,0:T(8,128)}, bf16[512,4096]{1,0:T(8,128)(2,1)}) custom-call(s32[1]{0:T(128)} %bitcast.20.where, bf16[1024,512]{1,0:T(8,128)(2,1)} %copy-done.7, bf16[1024,512]{1,0:T(8,128)(2,1)} %copy-done.9, bf16[1024,512]{1,0:T(8,128)(2,1)} %copy-done.7, bf16[1024,512]{1,0:T(8,128)(2,1)} %copy-done.9, bf16[1024,512]{1,0:T(8,128)(2,1)} %copy-done.10, ...), custom_call_target="tpu_custom_call" | custom-call | tf_op jit(solution)/shard_map/update/pallas_call | solution.py:441
  434.7 8.7 %update.6 = (f32[512,3072]{1,0:T(8,128)}, bf16[512,3072]{1,0:T(8,128)(2,1)}) custom-call(s32[1]{0:T(128)} %bitcast.20.where, bf16[1024,512]{1,0:T(8,128)(2,1)} %copy-done.4, bf16[1024,512]{1,0:T(8,128)(2,1)} %copy-done.5, bf16[1024,512]{1,0:T(8,128)(2,1)} %copy-done.4, bf16[1024,512]{1,0:T(8,128)(2,1)} %copy-done.5, bf16[512,512]{1,0:T(8,128)(2,1)} %copy-done.39, ...), custom_call_target="tpu_custom_call" | custom-call | tf_op jit(solution)/shard_map/update/pallas_call | solution.py:441
  444.7 3.0 collective-permute-done.72
  459.9 3.3 update.7
  (559 shorter events, 221.2 us)
Async XLA Ops:
  7.8 40.3 %collective-permute-start = (bf16[12,512]{1,0:T(8,128)(2,1)}, bf16[12,512]{1,0:T(8,128)(2,1)}, u32[]{:S(2)}, u32[]{:S(2)}) collective-permute-start(bf16[12,512]{1,0:T(8,128)(2,1)} %get-tuple-element.356), channel_id=1, source_target_pairs={{0,1},{1,0},{2,3},{3,2},{4,5},{5,4},{6,7},{7,6},{8,9},{9,8},{10,11... | collective-permute-start | bytes 36872 | tf_op jit(solution)/shard_map/ppermute | solution.py:534
  8.5 42.4 %collective-permute-start.4 = (bf16[128,1024]{1,0:T(8,128)(2,1)}, bf16[128,1024]{1,0:T(8,128)(2,1)S(1)}, u32[]{:S(2)}, u32[]{:S(2)}) collective-permute-start(bf16[128,1024]{1,0:T(8,128)(2,1)} %cast.6.refs_1_), channel_id=1, source_target_pairs={{0,1},{1,0},{2,3},{3,2},{4,5},{5,4},{6,7},{7,6},{8,9},{9,8},{10,11... | collective-permute-start | bytes 786440 | tf_op jit(solution)/shard_map/ppermute | solution.py:553
  28.4 25.3 %collective-permute-start.7 = (bf16[128,2048]{1,0:T(8,128)(2,1)}, bf16[128,2048]{1,0:T(8,128)(2,1)}, u32[]{:S(2)}, u32[]{:S(2)}) collective-permute-start(bf16[128,2048]{1,0:T(8,128)(2,1)} %cast.7.refs_1_), channel_id=1, source_target_pairs={{0,1},{1,0},{2,3},{3,2},{4,5},{5,4},{6,7},{7,6},{8,9},{9,8},{10,11... | collective-permute-start | bytes 1572872 | tf_op jit(solution)/shard_map/ppermute | solution.py:553
  30.8 25.3 %collective-permute-start.10 = (bf16[128,2048]{1,0:T(8,128)(2,1)}, bf16[128,2048]{1,0:T(8,128)(2,1)}, u32[]{:S(2)}, u32[]{:S(2)}) collective-permute-start(bf16[128,2048]{1,0:T(8,128)(2,1)} %cast.8.refs_1_), channel_id=1, source_target_pairs={{0,1},{1,0},{2,3},{3,2},{4,5},{5,4},{6,7},{7,6},{8,9},{9,8},{10,11... | collective-permute-start | bytes 1572872 | tf_op jit(solution)/shard_map/ppermute | solution.py:553
  48.9 37.0 %collective-permute-start.13 = (bf16[512,1024]{1,0:T(8,128)(2,1)}, bf16[512,1024]{1,0:T(8,128)(2,1)}, u32[]{:S(2)}, u32[]{:S(2)}) collective-permute-start(bf16[512,1024]{1,0:T(8,128)(2,1)} %copy-done.37), channel_id=1, source_target_pairs={{0,1},{1,0},{2,3},{3,2},{4,5},{5,4},{6,7},{7,6},{8,9},{9,8},{10,11... | collective-permute-start | bytes 3145736 | tf_op jit(solution)/shard_map/ppermute | solution.py:553
  55.6 22.5 %collective-permute-start.8 = (bf16[128,2048]{1,0:T(8,128)(2,1)}, bf16[128,2048]{1,0:T(8,128)(2,1)}, u32[]{:S(2)}, u32[]{:S(2)}) collective-permute-start(bf16[128,2048]{1,0:T(8,128)(2,1)} %x_part.5), channel_id=1, source_target_pairs={{0,2},{2,0},{4,6},{6,4},{8,10},{10,8},{12,14},{14,12},{1,3},{3,1},... | collective-permute-start | bytes 1572872 | tf_op jit(solution)/shard_map/ppermute | solution.py:564
  58.3 24.9 %collective-permute-start.11 = (bf16[128,2048]{1,0:T(8,128)(2,1)}, bf16[128,2048]{1,0:T(8,128)(2,1)}, u32[]{:S(2)}, u32[]{:S(2)}) collective-permute-start(bf16[128,2048]{1,0:T(8,128)(2,1)} %x_part.6), channel_id=1, source_target_pairs={{0,2},{2,0},{4,6},{6,4},{8,10},{10,8},{12,14},{14,12},{1,3},{3,1},... | collective-permute-start | bytes 1572872 | tf_op jit(solution)/shard_map/ppermute | solution.py:564
  88.1 25.4 %collective-permute-start.14 = (bf16[512,1024]{1,0:T(8,128)(2,1)}, bf16[512,1024]{1,0:T(8,128)(2,1)}, u32[]{:S(2)}, u32[]{:S(2)}) collective-permute-start(bf16[512,1024]{1,0:T(8,128)(2,1)} %x_part.7), channel_id=1, source_target_pairs={{0,2},{2,0},{4,6},{6,4},{8,10},{10,8},{12,14},{14,12},{1,3},{3,1},... | collective-permute-start | bytes 3145736 | tf_op jit(solution)/shard_map/ppermute | solution.py:564
  124.5 25.1 %collective-permute-start.18 = (bf16[1024,512]{1,0:T(8,128)(2,1)S(1)}, bf16[1024,512]{1,0:T(8,128)(2,1)S(1)}, u32[]{:S(2)}, u32[]{:S(2)}) collective-permute-start(bf16[1024,512]{1,0:T(8,128)(2,1)S(1)} %get-tuple-element.162), channel_id=1, source_target_pairs={{0,1},{1,0},{2,3},{3,2},{4,5},{5,4},{6,7},{7,6},{8,9},{9,8},{10,11... | collective-permute-start | bytes 3145736 | tf_op jit(solution)/shard_map/ppermute | solution.py:816
  136.7 40.5 %collective-permute-start.19 = (bf16[2048,512]{1,0:T(8,128)(2,1)S(1)}, bf16[2048,512]{1,0:T(8,128)(2,1)S(1)}, u32[]{:S(2)}, u32[]{:S(2)}) collective-permute-start(bf16[2048,512]{1,0:T(8,128)(2,1)S(1)} %get-tuple-element.165), channel_id=1, source_target_pairs={{0,16},{16,0},{1,17},{17,1},{2,18},{18,2},{3,19},{19,3},{4,20},{20... | collective-permute-start | bytes 6291464 | tf_op jit(solution)/shard_map/ppermute | solution.py:719
  152.5 24.3 %collective-permute-start.20 = (bf16[1024,512]{1,0:T(8,128)(2,1)S(1)}, bf16[1024,512]{1,0:T(8,128)(2,1)S(1)}, u32[]{:S(2)}, u32[]{:S(2)}) collective-permute-start(bf16[1024,512]{1,0:T(8,128)(2,1)S(1)} %get-tuple-element.167), channel_id=1, source_target_pairs={{0,1},{1,0},{2,3},{3,2},{4,5},{5,4},{6,7},{7,6},{8,9},{9,8},{10,11... | collective-permute-start | bytes 3145736 | tf_op jit(solution)/shard_map/ppermute | solution.py:816
  153.2 24.0 %collective-permute-start.21 = (bf16[1024,512]{1,0:T(8,128)(2,1)S(1)}, bf16[1024,512]{1,0:T(8,128)(2,1)S(1)}, u32[]{:S(2)}, u32[]{:S(2)}) collective-permute-start(bf16[1024,512]{1,0:T(8,128)(2,1)S(1)} %get-tuple-element.168.refs_6_), channel_id=1, source_target_pairs={{0,2},{2,0},{4,6},{6,4},{8,10},{10,8},{12,14},{14,12},{1,3},{3,1},... | collective-permute-start | bytes 3145736 | tf_op jit(solution)/shard_map/ppermute | solution.py:818
  162.7 36.0 %collective-permute-start.23 = (bf16[2048,512]{1,0:T(8,128)(2,1)S(1)}, bf16[2048,512]{1,0:T(8,128)(2,1)S(1)}, u32[]{:S(2)}, u32[]{:S(2)}) collective-permute-start(bf16[2048,512]{1,0:T(8,128)(2,1)S(1)} %get-tuple-element.171), channel_id=1, source_target_pairs={{0,16},{16,0},{1,17},{17,1},{2,18},{18,2},{3,19},{19,3},{4,20},{20... | collective-permute-start | bytes 6291464 | tf_op jit(solution)/shard_map/ppermute | solution.py:719
  179.9 25.6 %collective-permute-start.24 = (bf16[1024,512]{1,0:T(8,128)(2,1)S(1)}, bf16[1024,512]{1,0:T(8,128)(2,1)S(1)}, u32[]{:S(2)}, u32[]{:S(2)}) collective-permute-start(bf16[1024,512]{1,0:T(8,128)(2,1)S(1)} %get-tuple-element.173), channel_id=1, source_target_pairs={{0,1},{1,0},{2,3},{3,2},{4,5},{5,4},{6,7},{7,6},{8,9},{9,8},{10,11... | collective-permute-start | bytes 3145736 | tf_op jit(solution)/shard_map/ppermute | solution.py:816
  181.4 25.3 %collective-permute-start.25 = (bf16[1024,512]{1,0:T(8,128)(2,1)S(1)}, bf16[1024,512]{1,0:T(8,128)(2,1)S(1)}, u32[]{:S(2)}, u32[]{:S(2)}) collective-permute-start(bf16[1024,512]{1,0:T(8,128)(2,1)S(1)} %get-tuple-element.174.refs_6_), channel_id=1, source_target_pairs={{0,2},{2,0},{4,6},{6,4},{8,10},{10,8},{12,14},{14,12},{1,3},{3,1},... | collective-permute-start | bytes 3145736 | tf_op jit(solution)/shard_map/ppermute | solution.py:818
  182.8 25.0 %collective-permute-start.26 = (bf16[1024,512]{1,0:T(8,128)(2,1)S(1)}, bf16[1024,512]{1,0:T(8,128)(2,1)S(1)}, u32[]{:S(2)}, u32[]{:S(2)}) collective-permute-start(bf16[1024,512]{1,0:T(8,128)(2,1)S(1)} %get-tuple-element.176), channel_id=1, source_target_pairs={{0,4},{12,8},{2,6},{14,10},{4,0},{8,12},{6,2},{10,14},{1,5},{13,9}... | collective-permute-start | bytes 3145736 | tf_op jit(solution)/shard_map/ppermute | solution.py:820
  198.6 34.9 %collective-permute-start.28 = (bf16[2048,512]{1,0:T(8,128)(2,1)S(1)}, bf16[2048,512]{1,0:T(8,128)(2,1)S(1)}, u32[]{:S(2)}, u32[]{:S(2)}) collective-permute-start(bf16[2048,512]{1,0:T(8,128)(2,1)S(1)} %get-tuple-element.181), channel_id=1, source_target_pairs={{0,16},{16,0},{1,17},{17,1},{2,18},{18,2},{3,19},{19,3},{4,20},{20... | collective-permute-start | bytes 6291464 | tf_op jit(solution)/shard_map/ppermute | solution.py:719
  208.7 24.2 %collective-permute-start.29 = (bf16[1024,512]{1,0:T(8,128)(2,1)S(1)}, bf16[1024,512]{1,0:T(8,128)(2,1)S(1)}, u32[]{:S(2)}, u32[]{:S(2)}) collective-permute-start(bf16[1024,512]{1,0:T(8,128)(2,1)S(1)} %get-tuple-element.184), channel_id=1, source_target_pairs={{0,1},{1,0},{2,3},{3,2},{4,5},{5,4},{6,7},{7,6},{8,9},{9,8},{10,11... | collective-permute-start | bytes 3145736 | tf_op jit(solution)/shard_map/ppermute | solution.py:816
  209.2 23.8 %collective-permute-start.30 = (bf16[1024,512]{1,0:T(8,128)(2,1)S(1)}, bf16[1024,512]{1,0:T(8,128)(2,1)S(1)}, u32[]{:S(2)}, u32[]{:S(2)}) collective-permute-start(bf16[1024,512]{1,0:T(8,128)(2,1)S(1)} %get-tuple-element.185.refs_6_), channel_id=1, source_target_pairs={{0,2},{2,0},{4,6},{6,4},{8,10},{10,8},{12,14},{14,12},{1,3},{3,1},... | collective-permute-start | bytes 3145736 | tf_op jit(solution)/shard_map/ppermute | solution.py:818
  209.9 23.6 %collective-permute-start.31 = (bf16[1024,512]{1,0:T(8,128)(2,1)S(1)}, bf16[1024,512]{1,0:T(8,128)(2,1)S(1)}, u32[]{:S(2)}, u32[]{:S(2)}) collective-permute-start(bf16[1024,512]{1,0:T(8,128)(2,1)S(1)} %get-tuple-element.187), channel_id=1, source_target_pairs={{0,4},{12,8},{2,6},{14,10},{4,0},{8,12},{6,2},{10,14},{1,5},{13,9}... | collective-permute-start | bytes 3145736 | tf_op jit(solution)/shard_map/ppermute | solution.py:820
  234.4 25.0 %collective-permute-start.33 = (bf16[1024,512]{1,0:T(8,128)(2,1)S(1)}, bf16[1024,512]{1,0:T(8,128)(2,1)S(1)}, u32[]{:S(2)}, u32[]{:S(2)}) collective-permute-start(bf16[1024,512]{1,0:T(8,128)(2,1)S(1)} %get-tuple-element.189), channel_id=1, source_target_pairs={{0,1},{1,0},{2,3},{3,2},{4,5},{5,4},{6,7},{7,6},{8,9},{9,8},{10,11... | collective-permute-start | bytes 3145736 | tf_op jit(solution)/shard_map/ppermute | solution.py:816
  235.9 23.8 %collective-permute-start.34 = (bf16[1024,512]{1,0:T(8,128)(2,1)S(1)}, bf16[1024,512]{1,0:T(8,128)(2,1)S(1)}, u32[]{:S(2)}, u32[]{:S(2)}) collective-permute-start(bf16[1024,512]{1,0:T(8,128)(2,1)S(1)} %get-tuple-element.190.refs_6_), channel_id=1, source_target_pairs={{0,2},{2,0},{4,6},{6,4},{8,10},{10,8},{12,14},{14,12},{1,3},{3,1},... | collective-permute-start | bytes 3145736 | tf_op jit(solution)/shard_map/ppermute | solution.py:818
  237.3 24.9 %collective-permute-start.35 = (bf16[1024,512]{1,0:T(8,128)(2,1)S(1)}, bf16[1024,512]{1,0:T(8,128)(2,1)S(1)}, u32[]{:S(2)}, u32[]{:S(2)}) collective-permute-start(bf16[1024,512]{1,0:T(8,128)(2,1)S(1)} %get-tuple-element.192), channel_id=1, source_target_pairs={{0,4},{12,8},{2,6},{14,10},{4,0},{8,12},{6,2},{10,14},{1,5},{13,9}... | collective-permute-start | bytes 3145736 | tf_op jit(solution)/shard_map/ppermute | solution.py:820
  244.5 41.6 %collective-permute-start.38 = (bf16[1024,512]{1,0:T(8,128)(2,1)}, bf16[1024,512]{1,0:T(8,128)(2,1)}, u32[]{:S(2)}, u32[]{:S(2)}) collective-permute-start(bf16[1024,512]{1,0:T(8,128)(2,1)} %get-tuple-element.198), channel_id=1, source_target_pairs={{0,16},{16,0},{1,17},{17,1},{2,18},{18,2},{3,19},{19,3},{4,20},{20... | collective-permute-start | bytes 3145736 | tf_op jit(solution)/shard_map/ppermute | solution.py:719
  268.3 23.1 %collective-permute-start.41 = (bf16[1024,512]{1,0:T(8,128)(2,1)}, bf16[1024,512]{1,0:T(8,128)(2,1)}, u32[]{:S(2)}, u32[]{:S(2)}) collective-permute-start(bf16[1024,512]{1,0:T(8,128)(2,1)} %get-tuple-element.204), channel_id=1, source_target_pairs={{0,4},{12,8},{2,6},{14,10},{4,0},{8,12},{6,2},{10,14},{1,5},{13,9}... | collective-permute-start | bytes 3145736 | tf_op jit(solution)/shard_map/ppermute | solution.py:820
  298.5 23.4 %collective-permute-start.45 = (bf16[1024,512]{1,0:T(8,128)(2,1)}, bf16[1024,512]{1,0:T(8,128)(2,1)}, u32[]{:S(2)}, u32[]{:S(2)}) collective-permute-start(bf16[1024,512]{1,0:T(8,128)(2,1)} %get-tuple-element.210), channel_id=1, source_target_pairs={{0,4},{12,8},{2,6},{14,10},{4,0},{8,12},{6,2},{10,14},{1,5},{13,9}... | collective-permute-start | bytes 3145736 | tf_op jit(solution)/shard_map/ppermute | solution.py:820
  303.9 29.2 %collective-permute-start.52 = (bf16[1024,512]{1,0:T(8,128)(2,1)}, bf16[1024,512]{1,0:T(8,128)(2,1)}, u32[]{:S(2)}, u32[]{:S(2)}) collective-permute-start(bf16[1024,512]{1,0:T(8,128)(2,1)} %get-tuple-element.224.mine.refs_4_.refs_6_), channel_id=1, source_target_pairs={{0,16},{16,0},{1,17},{17,1},{2,18},{18,2},{3,19},{19,3},{4,20},{20... | collective-permute-start | bytes 3145736 | tf_op jit(solution)/shard_map/ppermute | solution.py:825
  326.2 32.7 %collective-permute-start.49 = (bf16[512,512]{1,0:T(8,128)(2,1)}, bf16[512,512]{1,0:T(8,128)(2,1)}, u32[]{:S(2)}, u32[]{:S(2)}) collective-permute-start(bf16[512,512]{1,0:T(8,128)(2,1)} %get-tuple-element.218.refs_1_), channel_id=1, source_target_pairs={{0,2},{2,0},{4,6},{6,4},{8,10},{10,8},{12,14},{14,12},{1,3},{3,1},... | collective-permute-start | bytes 1572872 | tf_op jit(solution)/shard_map/ppermute | solution.py:818
  327.6 31.3 %collective-permute-start.50 = (bf16[1024,512]{1,0:T(8,128)(2,1)}, bf16[1024,512]{1,0:T(8,128)(2,1)}, u32[]{:S(2)}, u32[]{:S(2)}) collective-permute-start(bf16[1024,512]{1,0:T(8,128)(2,1)} %get-tuple-element.220), channel_id=1, source_target_pairs={{0,4},{12,8},{2,6},{14,10},{4,0},{8,12},{6,2},{10,14},{1,5},{13,9}... | collective-permute-start | bytes 3145736 | tf_op jit(solution)/shard_map/ppermute | solution.py:820
  331.3 27.6 %collective-permute-start.51 = (bf16[1024,512]{1,0:T(8,128)(2,1)}, bf16[1024,512]{1,0:T(8,128)(2,1)}, u32[]{:S(2)}, u32[]{:S(2)}) collective-permute-start(bf16[1024,512]{1,0:T(8,128)(2,1)} %get-tuple-element.221.refs_5_), channel_id=1, source_target_pairs={{4,8},{8,4},{6,10},{10,6},{5,9},{9,5},{7,11},{11,7},{20,24},{24,20... | collective-permute-start | bytes 3145736 | tf_op jit(solution)/shard_map/ppermute | solution.py:822
  344.6 25.5 %collective-permute-start.57 = (bf16[1024,512]{1,0:T(8,128)(2,1)S(1)}, bf16[1024,512]{1,0:T(8,128)(2,1)S(1)}, u32[]{:S(2)}, u32[]{:S(2)}) collective-permute-start(bf16[1024,512]{1,0:T(8,128)(2,1)S(1)} %get-tuple-element.236.mine.refs_0_.refs_2_), channel_id=1, source_target_pairs={{0,16},{16,0},{1,17},{17,1},{2,18},{18,2},{3,19},{19,3},{4,20},{20... | collective-permute-start | bytes 3145736 | tf_op jit(solution)/shard_map/ppermute | solution.py:825
  365.5 25.5 %collective-permute-start.55 = (bf16[1024,512]{1,0:T(8,128)(2,1)}, bf16[1024,512]{1,0:T(8,128)(2,1)}, u32[]{:S(2)}, u32[]{:S(2)}) collective-permute-start(bf16[1024,512]{1,0:T(8,128)(2,1)} %get-tuple-element.232), channel_id=1, source_target_pairs={{0,4},{12,8},{2,6},{14,10},{4,0},{8,12},{6,2},{10,14},{1,5},{13,9}... | collective-permute-start | bytes 3145736 | tf_op jit(solution)/shard_map/ppermute | solution.py:820
  (182 other events, 1607.5 us)

commit v2 on v1

--- a/solution.py
+++ b/solution.py
@@ -508,7 +508,7 @@
     z_out = tuple((z * 2 + x, w * 2 + x) for x in range(2) for z, w in ((1, 0), (2, 3)))
     z_swap = z_in + z_out
     planes = [[z * 2, z * 2 + 1, 8 + z * 2, 8 + z * 2 + 1] for z in range(4)]
-    sizes = (2, 2, 2, 2, 2, 1, 1)
+    sizes = (2, 2, 2, 2, 2, 2)
 
     def __init__(self, share):
         self.core = lax.axis_index("res")
@@ -1038,6 +1038,7 @@
     grad_projected = attend_back(segment, projected, grad_mixed)
     qkv_grad = comm.push(False, normed, grad_projected)
     out_grad = comm.push(False, mixed, grad_branch)
+    comm.step()
     grad_normed = lax.optimization_barrier(comm.back_project(grad_projected))
     grad_tokens_part, grad_gain_one, grad_shift_one = norm_back_one(grad_normed)
     grad_tokens = grad_middle + grad_tokens_part
@@ -1076,10 +1077,8 @@
     comm.vectors_step()
     comm.step()
     comm.vectors_step()
+    comm.vectors_step()
     qkv = comm.update(False, qkv_grad, weight_qkv, rows_qkv, cols_qkv, 0)
-    comm.require(comm.held_out(qkv[-1]), 11)
-    comm.step()
-    comm.vectors_step()
     grad_vec = comm.vectors_step().T
     moment_new = DECAY * moment_vec + (1.0 - DECAY) * (grad_vec * grad_vec + EPS_SQUARE)
     square_sum = comm.pair_sum(jnp.sum(vectors * vectors, axis=0))

time: 470 us -> 465 us (0.989)
    ppermute x7 -> x6, waiting for transfers between devices: 65.3 us -> 55.1 us  [step(): buffers['from_y', tick] = lax.ppermute(outs['for_y'], 'fsdp', SWAP)]
    ppermute x9 -> x8, waiting for transfers between devices: 15 us -> 24.2 us  [step(): buffers['from_swap', tick] = lax.ppermute(outs['swap'], 'dp', self.z_swap)]
    ppermute x7 -> x6, waiting for transfers between devices: 3.44 us -> 9.32 us  [step(): buffers['from_x', tick] = lax.ppermute(outs['for_x'], 'dp', self.x_pairs)]
    unnamed x284 -> x246, local copies, waits for them, and re-layouts: 26.3 us -> 22.3 us
    ppermute x7 -> x6, starting transfers between devices: 9.85 us -> 8.48 us  [step(): buffers['from_mid', tick] = lax.ppermute(outs['v2'], 'dp', self.z_mid)]
    ppermute x9 -> x8, starting transfers between devices: 23 us -> 24 us  [step(): buffers['from_swap', tick] = lax.ppermute(outs['swap'], 'dp', self.z_swap)]
    pallas_call x41 -> x39, Pallas kernels: 64.4 us -> 63.9 us  [call(): pl.pallas_call(body, in_specs=[pl.BlockSpec(memory_space=pltpu.SMEM)] * l...]
  transfers between devices with their start and end apart: 73 -> 67, of which waited for: 29 -> 26; matrix products, arithmetic and copies ran while one was open for 9% -> 9% of each run, Pallas kernels for 39% -> 38%
where the time goes in v2:
time: 465 us; the launch traced here: 458 us
  Pallas kernels  189 us (41%)
  waiting for transfers between devices  115 us (25%)
  starting transfers between devices  72.9 us (16%)
  local copies, waits for them, and re-layouts  39.2 us (8%)
  other arithmetic  29.4 us (6%)
  between operations  12.1 us (3%)
    pallas_call x39, Pallas kernels, call(): pl.pallas_call(body, in_specs=[pl.BlockSpec(memory_space=pltpu.SMEM)] * l...  63.9 us
    ppermute x6, waiting for transfers between devices, step(): buffers['from_y', tick] = lax.ppermute(outs['for_y'], 'fsdp', SWAP)  55.1 us
    pallas_call x4, Pallas kernels, update(): pl.pallas_call(partial(update_kernel, units), grid_spec=pltpu.PrefetchSca...  34.6 us
    pallas_call x12, Pallas kernels, finish(): pl.pallas_call(finish_kernel, grid_spec=pltpu.PrefetchScalarGridSpec(num_...  30.1 us
    pallas_call x4, Pallas kernels, forward_matmul(): pl.pallas_call(kernel, grid_spec=pltpu.PrefetchScalarGridSpec(num_scalar_...  29.3 us
    ppermute x8, waiting for transfers between devices, step(): buffers['from_swap', tick] = lax.ppermute(outs['swap'], 'dp', self.z_swap)  24.2 us
    ppermute x8, starting transfers between devices, step(): buffers['from_swap', tick] = lax.ppermute(outs['swap'], 'dp', self.z_swap)  24 us
    unnamed x246, local copies, waits for them, and re-layouts  22.3 us
  transfers between devices with their start and end apart: 67, of which 26 were waited for; matrix products, arithmetic and copies ran while one was open for 9% of the time, Pallas kernels for 38%

profile of v2, /device:TPU:0, one launch (start us, length us, event | category | flops | bytes accessed | tf_op | source)
XLA Modules:
  0.0 457.8 jit_solution(12790254809960007015)
XLA Ops:
  2.4 3.0 collective-permute-start.1
  10.5 13.2 %collective-permute-done.1.refs_2_.refs_0_ = bf16[128,3072]{1,0:T(8,128)(2,1)S(1)} collective-permute-done((bf16[128,3072]{1,0:T(8,128)(2,1)S(1)}, bf16[128,3072]{1,0:T(8,128)(2,1)S(1)}, u32[]{:S(2)}, u32[]{:S(2)}) %collective-permute-start.1) | collective-permute-done | bytes 786464 | tf_op jit(solution)/shard_map/ppermute | solution.py:553
  37.9 3.7 collective-permute-done.2.refs_1_
  61.7 7.3 %forward_matmul.4 = (bf16[256,3072]{1,0:T(8,128)(2,1)S(1)}, f32[8,3072]{1,0:T(8,128)S(1)}) custom-call(s32[2]{0:T(128)S(1)} %pad_add_fusion.where, bf16[256,1024]{1,0:T(8,128)(2,1)S(1)} %add_convert_fusion.1.act, f32[512,3072]{1,0:T(8,128)} %refs_6_.1, bf16[256,3072]{1,0:T(8,128)(2,1)S(1)} %core_part.5.refs_0_, bf16[256,3072]{1,0:T(8,128)(2,1)S(1)} %copy-done.18, ...), custom_call_target="tpu_custom_call" | custom-call | tf_op jit(solution)/shard_map/forward_matmul/pallas_call | solution.py:209
  79.7 3.5 collective-permute-done.11.refs_1_
  89.6 3.3 forward_matmul.5
  96.3 11.9 %forward_matmul.6 = (bf16[256,4096]{1,0:T(8,128)(2,1)S(1)}, f32[256,4096]{1,0:T(8,128)}, f32[8,4096]{1,0:T(8,128)S(1)}) custom-call(s32[2]{0:T(128)S(1)} %copy-done.72, bf16[256,1024]{1,0:T(8,128)(2,1)S(1)} %add_convert_fusion.act, f32[512,4096]{1,0:T(8,128)} %refs_8_.3, bf16[256,2048]{1,0:T(8,128)(2,1)S(1)} %core_part.7.refs_3_.refs_0_, ...), custom_call_target="tpu_custom_call" | custom-call | tf_op jit(solution)/shard_map/forward_matmul/pallas_call | solution.py:209
  125.9 10.0 %slope_matmul.1.grad = bf16[256,4096]{1,0:T(8,128)(2,1)S(1)} custom-call(s32[2]{0:T(128)S(1)} %copy-done.73, bf16[256,1024]{1,0:T(8,128)(2,1)S(1)} %copy-done.28, f32[2048,1024]{1,0:T(8,128)} %refs_8_.2, bf16[1024,1024]{1,0:T(8,128)(2,1)S(1)} %core_part.9.refs_0_.half, bf16[1024,1024]{1,0:T(8,128)(2,1)} %collective-permute-done.15.refs_1_.other, ...), custom_call_target="tpu_custom_call" | custom-call | tf_op jit(solution)/shard_map/slope_matmul/pallas_call | solution.py:319
  137.7 13.3 %collective-permute-done.18.refs_5_ = bf16[1024,512]{1,0:T(8,128)(2,1)S(1)} collective-permute-done((bf16[1024,512]{1,0:T(8,128)(2,1)S(1)}, bf16[1024,512]{1,0:T(8,128)(2,1)S(1)}, u32[]{:S(2)}, u32[]{:S(2)}) %collective-permute-start.18) | collective-permute-done | bytes 1048608 | tf_op jit(solution)/shard_map/ppermute | solution.py:816
  156.3 6.9 %forward_matmul.7 = (bf16[256,1024]{1,0:T(8,128)(2,1)}, f32[8,1024]{1,0:T(8,128)S(1)}) custom-call(s32[2]{0:T(128)S(1)} %copy-done.73, bf16[256,4096]{1,0:T(8,128)(2,1)S(1)} %copy-done.1, f32[2048,1024]{1,0:T(8,128)} %refs_8_.2, bf16[1024,1024]{1,0:T(8,128)(2,1)S(1)} %core_part.9.refs_0_.half, bf16[1024,1024]{1,0:T(8,128)(2,1)} %collective-permute-done.15.refs_1_.other, ...), custom_call_target="tpu_custom_call" | custom-call | tf_op jit(solution)/shard_map/forward_matmul/pallas_call | solution.py:209
  163.2 9.8 %backward_matmul.3 = f32[256,1024]{1,0:T(8,128)S(1)} custom-call(s32[2]{0:T(128)S(1)} %copy-done.73, bf16[256,4096]{1,0:T(8,128)(2,1)S(1)} %slope_matmul.1.grad, f32[512,4096]{1,0:T(8,128)} %refs_8_.3, bf16[256,2048]{1,0:T(8,128)(2,1)S(1)} %copy-done.12, bf16[256,2048]{1,0:T(8,128)(2,1)} %collective-permute-done.9.refs_1_, bf16[256,2048]{1,0:T(8,128)(2,1)S(1)} %copy-done.21, ...), custom_call_target="tpu_custom_call" | custom-call | tf_op jit(solution)/shard_map/backward_matmul/pallas_call | solution.py:275
  173.8 4.7 %collective-permute-done.20.refs_5_ = bf16[1024,512]{1,0:T(8,128)(2,1)S(1)} collective-permute-done((bf16[1024,512]{1,0:T(8,128)(2,1)S(1)}, bf16[1024,512]{1,0:T(8,128)(2,1)S(1)}, u32[]{:S(2)}, u32[]{:S(2)}) %collective-permute-start.20) | collective-permute-done | bytes 1048608 | tf_op jit(solution)/shard_map/ppermute | solution.py:816
  186.3 3.8 backward_matmul.4.refs_3_
  190.2 9.0 %attend_back.1.grad = bf16[256,3072]{1,0:T(8,128)(2,1)S(1)} custom-call(s32[256,1]{1,0:T(8,128)S(1)} %fusion.2.refs_0_, s32[1,256]{1,0:T(1,128)S(1)} %copy-done.79, bf16[256,3072]{1,0:T(8,128)(2,1)S(1)} %copy-done.14, bf16[256,1024]{1,0:T(8,128)(2,1)S(1)} %backward_matmul.4.refs_3_), custom_call_target="tpu_custom_call" | custom-call | flops 1 | bytes 1 | tf_op jit(solution)/shard_map/attend_back/pallas_call | solution.py:475
  200.8 4.0 collective-permute-done.24.refs_5_
  214.0 15.3 %collective-permute-done.29.refs_5_ = bf16[1024,512]{1,0:T(8,128)(2,1)S(1)} collective-permute-done((bf16[1024,512]{1,0:T(8,128)(2,1)S(1)}, bf16[1024,512]{1,0:T(8,128)(2,1)S(1)}, u32[]{:S(2)}, u32[]{:S(2)}) %collective-permute-start.29) | collective-permute-done | bytes 1048608 | tf_op jit(solution)/shard_map/ppermute | solution.py:816
  234.0 4.6 %collective-permute-start.35 = (bf16[1024,512]{1,0:T(8,128)(2,1)S(1)}, bf16[1024,512]{1,0:T(8,128)(2,1)S(1)}, u32[]{:S(2)}, u32[]{:S(2)}) collective-permute-start(bf16[1024,512]{1,0:T(8,128)(2,1)S(1)} %get-tuple-element.181), channel_id=1, source_target_pairs={{0,4},{12,8},{2,6},{14,10},{4,0},{8,12},{6,2},{10,14},{1,5},{13,9}... | collective-permute-start | bytes 3145736 | tf_op jit(solution)/shard_map/ppermute | solution.py:820
  239.3 16.6 %collective-permute-done.33.refs_5_ = bf16[1024,512]{1,0:T(8,128)(2,1)S(1)} collective-permute-done((bf16[1024,512]{1,0:T(8,128)(2,1)S(1)}, bf16[1024,512]{1,0:T(8,128)(2,1)S(1)}, u32[]{:S(2)}, u32[]{:S(2)}) %collective-permute-start.33) | collective-permute-done | bytes 1048608 | tf_op jit(solution)/shard_map/ppermute | solution.py:816
  257.5 3.1 t.16
  264.5 4.6 %collective-permute-start.40 = (bf16[1024,512]{1,0:T(8,128)(2,1)}, bf16[1024,512]{1,0:T(8,128)(2,1)}, u32[]{:S(2)}, u32[]{:S(2)}) collective-permute-start(bf16[1024,512]{1,0:T(8,128)(2,1)} %get-tuple-element.190), channel_id=1, source_target_pairs={{0,4},{12,8},{2,6},{14,10},{4,0},{8,12},{6,2},{10,14},{1,5},{13,9}... | collective-permute-start | bytes 3145736 | tf_op jit(solution)/shard_map/ppermute | solution.py:820
  274.9 7.7 %backward_matmul.5 = f32[256,1024]{1,0:T(8,128)S(1)} custom-call(s32[2]{0:T(128)S(1)} %copy-done.73, bf16[256,3072]{1,0:T(8,128)(2,1)S(1)} %attend_back.1.grad, f32[512,3072]{1,0:T(8,128)} %refs_6_.1, bf16[256,3072]{1,0:T(8,128)(2,1)S(1)} %copy-done.16, bf16[256,3072]{1,0:T(8,128)(2,1)S(1)} %copy-done.19, f32[8,128]{1,0:T(8,128)S(1)} %collective-permute-done.37.refs_2_), custom_call_target="tpu_custom_call" | custom-call | tf_op jit(solution)/shard_map/backward_matmul/pallas_call | solution.py:275
  288.3 5.3 %t.17 = (bf16[1024,512]{1,0:T(8,128)(2,1)S(1)}, bf16[1024,512]{1,0:T(8,128)(2,1)S(1)}, bf16[1024,512]{1,0:T(8,128)(2,1)}, bf16[1024,512]{1,0:T(8,128)(2,1)S(1)},...) custom-call(s32[1]{0:T(128)} %bitcast.16.refs_0_, bf16[1024,512]{1,0:T(8,128)(2,1)S(1)} %copy-done.55, ...), custom_call_target="tpu_custom_call" | custom-call | flops 1 | bytes 1 | tf_op jit(solution)/shard_map/t/pallas_call | solution.py:475
  297.3 3.6 collective-permute-start.43
  311.9 5.2 %collective-permute-done.42.refs_2_ = bf16[1024,512]{1,0:T(8,128)(2,1)} collective-permute-done((bf16[1024,512]{1,0:T(8,128)(2,1)S(1)}, bf16[1024,512]{1,0:T(8,128)(2,1)}, u32[]{:S(2)}, u32[]{:S(2)}) %collective-permute-start.42) | collective-permute-done | bytes 1048608 | tf_op jit(solution)/shard_map/ppermute | solution.py:818
  319.2 4.0 t.18
  323.1 3.7 collective-permute-start.47
  343.1 11.3 %update.4 = (f32[2048,1024]{1,0:T(8,128)}, bf16[2048,1024]{1,0:T(8,128)(2,1)}) custom-call(s32[1]{0:T(128)} %bitcast.20.where, bf16[1024,512]{1,0:T(8,128)(2,1)} %copy-done.4, bf16[1024,512]{1,0:T(8,128)(2,1)} %collective-permute-done.45.theirs.refs_1_.refs_3_, bf16[1024,512]{1,0:T(8,128)(2,1)} %copy-done.4, ...), custom_call_target="tpu_custom_call" | custom-call | tf_op jit(solution)/shard_map/update/pallas_call | solution.py:441
  354.5 3.5 t.19
  368.3 17.4 %collective-permute-done.53.refs_4_ = bf16[1024,512]{1,0:T(8,128)(2,1)} collective-permute-done((bf16[1024,512]{1,0:T(8,128)(2,1)}, bf16[1024,512]{1,0:T(8,128)(2,1)}, u32[]{:S(2)}, u32[]{:S(2)}) %collective-permute-start.53) | collective-permute-done | bytes 1048608 | tf_op jit(solution)/shard_map/ppermute | solution.py:820
  405.7 11.3 %update.5 = (f32[512,4096]{1,0:T(8,128)}, bf16[512,4096]{1,0:T(8,128)(2,1)}) custom-call(s32[1]{0:T(128)} %bitcast.20.where, bf16[1024,512]{1,0:T(8,128)(2,1)} %copy-done.5, bf16[1024,512]{1,0:T(8,128)(2,1)} %copy-done.6, bf16[1024,512]{1,0:T(8,128)(2,1)} %copy-done.5, bf16[1024,512]{1,0:T(8,128)(2,1)} %copy-done.6, ...), custom_call_target="tpu_custom_call" | custom-call | tf_op jit(solution)/shard_map/update/pallas_call | solution.py:441
  442.8 3.3 update.7
  448.9 8.7 %update.6 = (f32[512,3072]{1,0:T(8,128)}, bf16[512,3072]{1,0:T(8,128)(2,1)}) custom-call(s32[1]{0:T(128)} %bitcast.20.where, bf16[1024,512]{1,0:T(8,128)(2,1)} %copy-done.9, bf16[1024,512]{1,0:T(8,128)(2,1)} %collective-permute-done.61.theirs.refs_1_.refs_3_, bf16[1024,512]{1,0:T(8,128)(2,1)} %copy-done.9, ...), custom_call_target="tpu_custom_call" | custom-call | tf_op jit(solution)/shard_map/update/pallas_call | solution.py:441
  (507 shorter events, 209.1 us)
Async XLA Ops:
  7.8 40.3 %collective-permute-start = (bf16[12,512]{1,0:T(8,128)(2,1)}, bf16[12,512]{1,0:T(8,128)(2,1)}, u32[]{:S(2)}, u32[]{:S(2)}) collective-permute-start(bf16[12,512]{1,0:T(8,128)(2,1)} %get-tuple-element.334), channel_id=1, source_target_pairs={{0,1},{1,0},{2,3},{3,2},{4,5},{5,4},{6,7},{7,6},{8,9},{9,8},{10,11... | collective-permute-start | bytes 36872 | tf_op jit(solution)/shard_map/ppermute | solution.py:534
  8.5 42.4 %collective-permute-start.4 = (bf16[128,1024]{1,0:T(8,128)(2,1)}, bf16[128,1024]{1,0:T(8,128)(2,1)S(1)}, u32[]{:S(2)}, u32[]{:S(2)}) collective-permute-start(bf16[128,1024]{1,0:T(8,128)(2,1)} %cast.6.refs_1_), channel_id=1, source_target_pairs={{0,1},{1,0},{2,3},{3,2},{4,5},{5,4},{6,7},{7,6},{8,9},{9,8},{10,11... | collective-permute-start | bytes 786440 | tf_op jit(solution)/shard_map/ppermute | solution.py:553
  28.4 25.3 %collective-permute-start.7 = (bf16[128,2048]{1,0:T(8,128)(2,1)}, bf16[128,2048]{1,0:T(8,128)(2,1)}, u32[]{:S(2)}, u32[]{:S(2)}) collective-permute-start(bf16[128,2048]{1,0:T(8,128)(2,1)} %cast.7.refs_1_), channel_id=1, source_target_pairs={{0,1},{1,0},{2,3},{3,2},{4,5},{5,4},{6,7},{7,6},{8,9},{9,8},{10,11... | collective-permute-start | bytes 1572872 | tf_op jit(solution)/shard_map/ppermute | solution.py:553
  30.8 25.3 %collective-permute-start.10 = (bf16[128,2048]{1,0:T(8,128)(2,1)}, bf16[128,2048]{1,0:T(8,128)(2,1)}, u32[]{:S(2)}, u32[]{:S(2)}) collective-permute-start(bf16[128,2048]{1,0:T(8,128)(2,1)} %cast.8.refs_1_), channel_id=1, source_target_pairs={{0,1},{1,0},{2,3},{3,2},{4,5},{5,4},{6,7},{7,6},{8,9},{9,8},{10,11... | collective-permute-start | bytes 1572872 | tf_op jit(solution)/shard_map/ppermute | solution.py:553
  48.8 37.0 %collective-permute-start.13 = (bf16[512,1024]{1,0:T(8,128)(2,1)}, bf16[512,1024]{1,0:T(8,128)(2,1)}, u32[]{:S(2)}, u32[]{:S(2)}) collective-permute-start(bf16[512,1024]{1,0:T(8,128)(2,1)} %copy-done.35), channel_id=1, source_target_pairs={{0,1},{1,0},{2,3},{3,2},{4,5},{5,4},{6,7},{7,6},{8,9},{9,8},{10,11... | collective-permute-start | bytes 3145736 | tf_op jit(solution)/shard_map/ppermute | solution.py:553
  55.6 22.5 %collective-permute-start.8 = (bf16[128,2048]{1,0:T(8,128)(2,1)}, bf16[128,2048]{1,0:T(8,128)(2,1)}, u32[]{:S(2)}, u32[]{:S(2)}) collective-permute-start(bf16[128,2048]{1,0:T(8,128)(2,1)} %x_part.5), channel_id=1, source_target_pairs={{0,2},{2,0},{4,6},{6,4},{8,10},{10,8},{12,14},{14,12},{1,3},{3,1},... | collective-permute-start | bytes 1572872 | tf_op jit(solution)/shard_map/ppermute | solution.py:564
  58.3 24.9 %collective-permute-start.11 = (bf16[128,2048]{1,0:T(8,128)(2,1)}, bf16[128,2048]{1,0:T(8,128)(2,1)}, u32[]{:S(2)}, u32[]{:S(2)}) collective-permute-start(bf16[128,2048]{1,0:T(8,128)(2,1)} %x_part.6), channel_id=1, source_target_pairs={{0,2},{2,0},{4,6},{6,4},{8,10},{10,8},{12,14},{14,12},{1,3},{3,1},... | collective-permute-start | bytes 1572872 | tf_op jit(solution)/shard_map/ppermute | solution.py:564
  88.1 26.3 %collective-permute-start.14 = (bf16[512,1024]{1,0:T(8,128)(2,1)}, bf16[512,1024]{1,0:T(8,128)(2,1)}, u32[]{:S(2)}, u32[]{:S(2)}) collective-permute-start(bf16[512,1024]{1,0:T(8,128)(2,1)} %x_part.7), channel_id=1, source_target_pairs={{0,2},{2,0},{4,6},{6,4},{8,10},{10,8},{12,14},{14,12},{1,3},{3,1},... | collective-permute-start | bytes 3145736 | tf_op jit(solution)/shard_map/ppermute | solution.py:564
  125.3 25.6 %collective-permute-start.18 = (bf16[1024,512]{1,0:T(8,128)(2,1)S(1)}, bf16[1024,512]{1,0:T(8,128)(2,1)S(1)}, u32[]{:S(2)}, u32[]{:S(2)}) collective-permute-start(bf16[1024,512]{1,0:T(8,128)(2,1)S(1)} %get-tuple-element.151), channel_id=1, source_target_pairs={{0,1},{1,0},{2,3},{3,2},{4,5},{5,4},{6,7},{7,6},{8,9},{9,8},{10,11... | collective-permute-start | bytes 3145736 | tf_op jit(solution)/shard_map/ppermute | solution.py:816
  137.4 41.4 %collective-permute-start.19 = (bf16[2048,512]{1,0:T(8,128)(2,1)S(1)}, bf16[2048,512]{1,0:T(8,128)(2,1)S(1)}, u32[]{:S(2)}, u32[]{:S(2)}) collective-permute-start(bf16[2048,512]{1,0:T(8,128)(2,1)S(1)} %get-tuple-element.154), channel_id=1, source_target_pairs={{0,16},{16,0},{1,17},{17,1},{2,18},{18,2},{3,19},{19,3},{4,20},{20... | collective-permute-start | bytes 6291464 | tf_op jit(solution)/shard_map/ppermute | solution.py:719
  153.7 24.8 %collective-permute-start.20 = (bf16[1024,512]{1,0:T(8,128)(2,1)S(1)}, bf16[1024,512]{1,0:T(8,128)(2,1)S(1)}, u32[]{:S(2)}, u32[]{:S(2)}) collective-permute-start(bf16[1024,512]{1,0:T(8,128)(2,1)S(1)} %get-tuple-element.156), channel_id=1, source_target_pairs={{0,1},{1,0},{2,3},{3,2},{4,5},{5,4},{6,7},{7,6},{8,9},{9,8},{10,11... | collective-permute-start | bytes 3145736 | tf_op jit(solution)/shard_map/ppermute | solution.py:816
  154.3 24.5 %collective-permute-start.21 = (bf16[1024,512]{1,0:T(8,128)(2,1)S(1)}, bf16[1024,512]{1,0:T(8,128)(2,1)S(1)}, u32[]{:S(2)}, u32[]{:S(2)}) collective-permute-start(bf16[1024,512]{1,0:T(8,128)(2,1)S(1)} %get-tuple-element.157.refs_6_), channel_id=1, source_target_pairs={{0,2},{2,0},{4,6},{6,4},{8,10},{10,8},{12,14},{14,12},{1,3},{3,1},... | collective-permute-start | bytes 3145736 | tf_op jit(solution)/shard_map/ppermute | solution.py:818
  156.2 44.6 %collective-permute-start.23 = (bf16[2048,512]{1,0:T(8,128)(2,1)S(1)}, bf16[2048,512]{1,0:T(8,128)(2,1)S(1)}, u32[]{:S(2)}, u32[]{:S(2)}) collective-permute-start(bf16[2048,512]{1,0:T(8,128)(2,1)S(1)} %get-tuple-element.160), channel_id=1, source_target_pairs={{0,16},{16,0},{1,17},{17,1},{2,18},{18,2},{3,19},{19,3},{4,20},{20... | collective-permute-start | bytes 6291464 | tf_op jit(solution)/shard_map/ppermute | solution.py:719
  181.1 23.7 %collective-permute-start.24 = (bf16[1024,512]{1,0:T(8,128)(2,1)S(1)}, bf16[1024,512]{1,0:T(8,128)(2,1)S(1)}, u32[]{:S(2)}, u32[]{:S(2)}) collective-permute-start(bf16[1024,512]{1,0:T(8,128)(2,1)S(1)} %get-tuple-element.162), channel_id=1, source_target_pairs={{0,1},{1,0},{2,3},{3,2},{4,5},{5,4},{6,7},{7,6},{8,9},{9,8},{10,11... | collective-permute-start | bytes 3145736 | tf_op jit(solution)/shard_map/ppermute | solution.py:816
  182.7 23.3 %collective-permute-start.25 = (bf16[1024,512]{1,0:T(8,128)(2,1)S(1)}, bf16[1024,512]{1,0:T(8,128)(2,1)S(1)}, u32[]{:S(2)}, u32[]{:S(2)}) collective-permute-start(bf16[1024,512]{1,0:T(8,128)(2,1)S(1)} %get-tuple-element.163.refs_6_), channel_id=1, source_target_pairs={{0,2},{2,0},{4,6},{6,4},{8,10},{10,8},{12,14},{14,12},{1,3},{3,1},... | collective-permute-start | bytes 3145736 | tf_op jit(solution)/shard_map/ppermute | solution.py:818
  183.2 23.0 %collective-permute-start.26 = (bf16[1024,512]{1,0:T(8,128)(2,1)S(1)}, bf16[1024,512]{1,0:T(8,128)(2,1)S(1)}, u32[]{:S(2)}, u32[]{:S(2)}) collective-permute-start(bf16[1024,512]{1,0:T(8,128)(2,1)S(1)} %get-tuple-element.165), channel_id=1, source_target_pairs={{0,4},{12,8},{2,6},{14,10},{4,0},{8,12},{6,2},{10,14},{1,5},{13,9}... | collective-permute-start | bytes 3145736 | tf_op jit(solution)/shard_map/ppermute | solution.py:820
  200.6 30.4 %collective-permute-start.28 = (bf16[2048,512]{1,0:T(8,128)(2,1)S(1)}, bf16[2048,512]{1,0:T(8,128)(2,1)S(1)}, u32[]{:S(2)}, u32[]{:S(2)}) collective-permute-start(bf16[2048,512]{1,0:T(8,128)(2,1)S(1)} %get-tuple-element.170), channel_id=1, source_target_pairs={{0,16},{16,0},{1,17},{17,1},{2,18},{18,2},{3,19},{19,3},{4,20},{20... | collective-permute-start | bytes 6291464 | tf_op jit(solution)/shard_map/ppermute | solution.py:719
  207.0 22.3 %collective-permute-start.29 = (bf16[1024,512]{1,0:T(8,128)(2,1)S(1)}, bf16[1024,512]{1,0:T(8,128)(2,1)S(1)}, u32[]{:S(2)}, u32[]{:S(2)}) collective-permute-start(bf16[1024,512]{1,0:T(8,128)(2,1)S(1)} %get-tuple-element.173), channel_id=1, source_target_pairs={{0,1},{1,0},{2,3},{3,2},{4,5},{5,4},{6,7},{7,6},{8,9},{9,8},{10,11... | collective-permute-start | bytes 3145736 | tf_op jit(solution)/shard_map/ppermute | solution.py:816
  232.0 23.9 %collective-permute-start.33 = (bf16[1024,512]{1,0:T(8,128)(2,1)S(1)}, bf16[1024,512]{1,0:T(8,128)(2,1)S(1)}, u32[]{:S(2)}, u32[]{:S(2)}) collective-permute-start(bf16[1024,512]{1,0:T(8,128)(2,1)S(1)} %get-tuple-element.178), channel_id=1, source_target_pairs={{0,1},{1,0},{2,3},{3,2},{4,5},{5,4},{6,7},{7,6},{8,9},{9,8},{10,11... | collective-permute-start | bytes 3145736 | tf_op jit(solution)/shard_map/ppermute | solution.py:816
  233.5 22.9 %collective-permute-start.34 = (bf16[1024,512]{1,0:T(8,128)(2,1)S(1)}, bf16[1024,512]{1,0:T(8,128)(2,1)S(1)}, u32[]{:S(2)}, u32[]{:S(2)}) collective-permute-start(bf16[1024,512]{1,0:T(8,128)(2,1)S(1)} %get-tuple-element.179.refs_6_), channel_id=1, source_target_pairs={{0,2},{2,0},{4,6},{6,4},{8,10},{10,8},{12,14},{14,12},{1,3},{3,1},... | collective-permute-start | bytes 3145736 | tf_op jit(solution)/shard_map/ppermute | solution.py:818
  234.0 23.5 %collective-permute-start.35 = (bf16[1024,512]{1,0:T(8,128)(2,1)S(1)}, bf16[1024,512]{1,0:T(8,128)(2,1)S(1)}, u32[]{:S(2)}, u32[]{:S(2)}) collective-permute-start(bf16[1024,512]{1,0:T(8,128)(2,1)S(1)} %get-tuple-element.181), channel_id=1, source_target_pairs={{0,4},{12,8},{2,6},{14,10},{4,0},{8,12},{6,2},{10,14},{1,5},{13,9}... | collective-permute-start | bytes 3145736 | tf_op jit(solution)/shard_map/ppermute | solution.py:820
  264.0 22.1 %collective-permute-start.39 = (bf16[1024,512]{1,0:T(8,128)(2,1)}, bf16[1024,512]{1,0:T(8,128)(2,1)}, u32[]{:S(2)}, u32[]{:S(2)}) collective-permute-start(bf16[1024,512]{1,0:T(8,128)(2,1)} %get-tuple-element.188.refs_4_), channel_id=1, source_target_pairs={{0,2},{2,0},{4,6},{6,4},{8,10},{10,8},{12,14},{14,12},{1,3},{3,1},... | collective-permute-start | bytes 3145736 | tf_op jit(solution)/shard_map/ppermute | solution.py:818
  264.5 23.7 %collective-permute-start.40 = (bf16[1024,512]{1,0:T(8,128)(2,1)}, bf16[1024,512]{1,0:T(8,128)(2,1)}, u32[]{:S(2)}, u32[]{:S(2)}) collective-permute-start(bf16[1024,512]{1,0:T(8,128)(2,1)} %get-tuple-element.190), channel_id=1, source_target_pairs={{0,4},{12,8},{2,6},{14,10},{4,0},{8,12},{6,2},{10,14},{1,5},{13,9}... | collective-permute-start | bytes 3145736 | tf_op jit(solution)/shard_map/ppermute | solution.py:820
  273.3 32.3 %collective-permute-start.45 = (bf16[1024,512]{1,0:T(8,128)(2,1)S(1)}, bf16[1024,512]{1,0:T(8,128)(2,1)}, u32[]{:S(2)}, u32[]{:S(2)}) collective-permute-start(bf16[1024,512]{1,0:T(8,128)(2,1)S(1)} %get-tuple-element.199.mine.refs_0_.refs_2_), channel_id=1, source_target_pairs={{0,16},{16,0},{1,17},{17,1},{2,18},{18,2},{3,19},{19,3},{4,20},{20... | collective-permute-start | bytes 3145736 | tf_op jit(solution)/shard_map/ppermute | solution.py:825
  302.6 26.0 %collective-permute-start.49 = (bf16[1024,512]{1,0:T(8,128)(2,1)}, bf16[1024,512]{1,0:T(8,128)(2,1)}, u32[]{:S(2)}, u32[]{:S(2)}) collective-permute-start(bf16[1024,512]{1,0:T(8,128)(2,1)} %get-tuple-element.208.mine.refs_4_.refs_6_), channel_id=1, source_target_pairs={{0,16},{16,0},{1,17},{17,1},{2,18},{18,2},{3,19},{19,3},{4,20},{20... | collective-permute-start | bytes 3145736 | tf_op jit(solution)/shard_map/ppermute | solution.py:825
  323.1 31.3 %collective-permute-start.47 = (bf16[1024,512]{1,0:T(8,128)(2,1)}, bf16[1024,512]{1,0:T(8,128)(2,1)}, u32[]{:S(2)}, u32[]{:S(2)}) collective-permute-start(bf16[1024,512]{1,0:T(8,128)(2,1)} %get-tuple-element.204), channel_id=1, source_target_pairs={{0,4},{12,8},{2,6},{14,10},{4,0},{8,12},{6,2},{10,14},{1,5},{13,9}... | collective-permute-start | bytes 3145736 | tf_op jit(solution)/shard_map/ppermute | solution.py:820
  326.8 27.6 %collective-permute-start.48 = (bf16[1024,512]{1,0:T(8,128)(2,1)}, bf16[1024,512]{1,0:T(8,128)(2,1)}, u32[]{:S(2)}, u32[]{:S(2)}) collective-permute-start(bf16[1024,512]{1,0:T(8,128)(2,1)} %get-tuple-element.205.refs_3_), channel_id=1, source_target_pairs={{4,8},{8,4},{6,10},{10,6},{5,9},{9,5},{7,11},{11,7},{20,24},{24,20... | collective-permute-start | bytes 3145736 | tf_op jit(solution)/shard_map/ppermute | solution.py:822
  338.6 26.0 %collective-permute-start.54 = (bf16[1024,512]{1,0:T(8,128)(2,1)S(1)}, bf16[1024,512]{1,0:T(8,128)(2,1)S(1)}, u32[]{:S(2)}, u32[]{:S(2)}) collective-permute-start(bf16[1024,512]{1,0:T(8,128)(2,1)S(1)} %get-tuple-element.219.mine.refs_0_.refs_2_), channel_id=1, source_target_pairs={{0,16},{16,0},{1,17},{17,1},{2,18},{18,2},{3,19},{19,3},{4,20},{20... | collective-permute-start | bytes 3145736 | tf_op jit(solution)/shard_map/ppermute | solution.py:825
  360.6 25.1 %collective-permute-start.53 = (bf16[1024,512]{1,0:T(8,128)(2,1)}, bf16[1024,512]{1,0:T(8,128)(2,1)}, u32[]{:S(2)}, u32[]{:S(2)}) collective-permute-start(bf16[1024,512]{1,0:T(8,128)(2,1)} %get-tuple-element.217), channel_id=1, source_target_pairs={{0,4},{12,8},{2,6},{14,10},{4,0},{8,12},{6,2},{10,14},{1,5},{13,9}... | collective-permute-start | bytes 3145736 | tf_op jit(solution)/shard_map/ppermute | solution.py:820
  363.3 28.1 %collective-permute-start.57 = (bf16[1024,512]{1,0:T(8,128)(2,1)}, bf16[1024,512]{1,0:T(8,128)(2,1)}, u32[]{:S(2)}, u32[]{:S(2)}) collective-permute-start(bf16[1024,512]{1,0:T(8,128)(2,1)} %get-tuple-element.226.mine.refs_4_.refs_6_), channel_id=1, source_target_pairs={{0,16},{16,0},{1,17},{17,1},{2,18},{18,2},{3,19},{19,3},{4,20},{20... | collective-permute-start | bytes 3145736 | tf_op jit(solution)/shard_map/ppermute | solution.py:825
  389.6 27.4 %collective-permute-start.56 = (bf16[1024,512]{1,0:T(8,128)(2,1)}, bf16[1024,512]{1,0:T(8,128)(2,1)}, u32[]{:S(2)}, u32[]{:S(2)}) collective-permute-start(bf16[1024,512]{1,0:T(8,128)(2,1)} %get-tuple-element.224), channel_id=1, source_target_pairs={{0,4},{12,8},{2,6},{14,10},{4,0},{8,12},{6,2},{10,14},{1,5},{13,9}... | collective-permute-start | bytes 3145736 | tf_op jit(solution)/shard_map/ppermute | solution.py:820
  401.6 22.4 %collective-permute-start.61 = (bf16[1024,512]{1,0:T(8,128)(2,1)S(1)}, bf16[1024,512]{1,0:T(8,128)(2,1)}, u32[]{:S(2)}, u32[]{:S(2)}) collective-permute-start(bf16[1024,512]{1,0:T(8,128)(2,1)S(1)} %get-tuple-element.234.mine.refs_0_.refs_2_), channel_id=1, source_target_pairs={{0,16},{16,0},{1,17},{17,1},{2,18},{18,2},{3,19},{19,3},{4,20},{20... | collective-permute-start | bytes 3145736 | tf_op jit(solution)/shard_map/ppermute | solution.py:825
  (157 other events, 1375.8 us)
